TPU v7x, 128 devices: a whole 4x4x4 slice. The times are simulated.
128 devices in a mesh: gx: 8 (over x, core), gy: 16 (over z, y).
Axes of the slice: x: 4, y: 4, z: 4, core: 2. Of those that a mesh axis runs over, the one named last changes fastest.
Arguments:
- enthalpy: float32 [160, 256, 1024], P(None, 'gy', 'gx'), may hold values from -6 to 6
- conduct_col: float32 [256, 1024], P('gy', 'gx'), may hold values from 0.5 to 40
- conduct_level: float32 [160], replicated, may hold values from 1 to 16
- surface_enthalpy: float32 [256, 1024], P('gy', 'gx'), may hold values from -6 to 6
- geothermal: float32 [256, 1024], P('gy', 'gx'), may hold values from 0.1 to 1
- melt_level: float32 [256, 1024], P('gy', 'gx'), may hold values from 0 to 0.5
- viscosity: float32 [256, 1024], P('gy', 'gx'), may hold values from 0.5 to 5
- drag: float32 [256, 1024], P('gy', 'gx'), may hold values from 0.05 to 0.5
- driving_stress: float32 [2, 256, 1024], P(None, 'gy', 'gx')
- ice_mask: int32 [256, 1024], P('gy', 'gx'), may hold values 0 or 1
- basin: int32 [256, 1024], P('gy', 'gx'), may hold values from 0 to 255, as said below
- owner_slot: int32 [256], replicated, may hold values from 0 to 255, each once
Outputs:
- enthalpy_next: float32 [160, 256, 1024], P(None, 'gy', 'gx')
- velocity: float32 [2, 256, 1024], P(None, 'gy', 'gx')
- basin_melt: float32 [256], P(('gx', 'gy'))
Inputs may be any that keep to these rules, and one draw needn't show every extreme that they name: `basin`: constant on aligned tiles of 32 x 32 columns; every basin holds the same number of tiles. `owner_slot`: each slot once.
All inputs are finite; a program needn't handle non-finite values. No bound on the sum of `ice_mask` on one device may be relied on, other than what follows from the above.
Results may differ from a plain program's by a relative error of at most 0.00028.
Values sent between devices are 32-bit elements; how exact they have to be, the bound alone decides.
No kernel may reach another device: no remote copies, remote signals or barrier semaphores. Data moves between devices by JAX's collectives and lax.ppermute only.
A program may use at most 128 MiB of HBM per device.

v0:
```python
import jax
import jax.numpy as jnp
from jax import lax
from jax.experimental import pallas as pl
from jax.experimental.pallas import tpu as pltpu
from jax.sharding import PartitionSpec as P

STEPS = 8
NZ = 160
ROWS = 16
LANES = 128
GROUPS = NZ // 8
SCALE = 16.0
WIDE = 144
BAND = 48
FULL = 60


def lane_ids(shape):
    return lax.broadcasted_iota(jnp.int32, shape, len(shape) - 1)


def row_ids(shape):
    return lax.broadcasted_iota(jnp.int32, shape, len(shape) - 2)


def turn(x, shift, axis):
    shift = shift % x.shape[axis]
    return x if shift == 0 else pltpu.roll(x, shift, axis)


def f32(*shape):
    return jax.ShapeDtypeStruct(shape, jnp.float32)


def call(kernel, outs, *args, places, scratch=(), limit=8, flops=0, aliases={}):
    spaces = {"v": pltpu.VMEM, "s": pltpu.SMEM, "a": pltpu.HBM}
    specs = [
        pl.BlockSpec(memory_space=spaces[p]) if p in spaces else pl.BlockSpec()
        for p in places
    ]
    size = sum(a.size * 4 for a in args) + sum(o.size * 4 for o in outs)
    return pl.pallas_call(
        kernel,
        out_shape=outs,
        in_specs=specs[: len(args)],
        out_specs=specs[len(args) :],
        scratch_shapes=list(scratch),
        input_output_aliases=aliases,
        compiler_params=pltpu.CompilerParams(vmem_limit_bytes=limit * 1024 * 1024),
        cost_estimate=pl.CostEstimate(
            flops=flops, bytes_accessed=size, transcendentals=0
        ),
    )(*args)


def rows_at(start, size):
    return pl.ds(pl.multiple_of(start, size if size in (8, 16) else 8), size)


def stencil(visc, drag, keep_e, keep_w, keep_n, keep_s):
    wide = visc.shape[1]
    tall = visc.shape[0]
    east = 0.5 * (visc + turn(visc, -1, 1) * keep_e)
    west = 0.5 * (visc + turn(visc, 1, 1) * keep_w)
    north = 0.5 * (visc + turn(visc, -1, 0) * keep_n)
    south = 0.5 * (visc + turn(visc, 1, 0) * keep_s)
    center = drag + east + west + north + south
    inv = 1.0 / SCALE
    center, east, west, north, south = (
        center * inv,
        east * keep_e * inv,
        west * keep_w * inv,
        north * keep_n * inv,
        south * keep_s * inv,
    )

    def apply(w):
        return (
            center * w
            - east * turn(w, -1, 1)
            - west * turn(w, 1, 1)
            - north * turn(w, -1, 0)
            - south * turn(w, 1, 0)
        )

    return apply


def edge_tile(tiles, first):
    lane = lane_ids((8, LANES))
    out = jnp.zeros((8, LANES), jnp.float32)
    for i in range(8):
        x = turn(tiles[i], 16 * i if first else 16 * i - 112, 1)
        out = jnp.where((lane >= 16 * i) & (lane < 16 * i + 16), x, out)
    return out


def fetch_all(pairs, sems):
    copies = [
        pltpu.make_async_copy(src, dst, sems.at[i]) for i, (src, dst) in enumerate(pairs)
    ]
    for copy in copies:
        copy.start()
    return copies


def wait_all(copies):
    for copy in copies:
        copy.wait()


def fields_kernel(stress_ref, visc_ref, drag_ref, f_ref, raw, out, sems):
    pairs = [(stress_ref, raw.at[pl.ds(0, 2)]), (visc_ref, raw.at[2]), (drag_ref, raw.at[3])]
    wait_all(fetch_all(pairs, sems))
    tiles = [raw[i // 2, 8 * (i % 2) : 8 * (i % 2) + 8, :] for i in range(8)]
    for i in range(8):
        out[i] = tiles[i]
    out[8] = edge_tile(tiles, True)
    out[9] = edge_tile(tiles, False)
    wait_all(fetch_all([(out, f_ref)], sems))


def transpose_kernel(
    e_ref, f_ref, lo_ref, hi_ref, first_ref, last_ref,
    buf, out, first, last, in_sems, out_sems,
):
    loads = [
        pltpu.make_async_copy(e_ref.at[:, pl.ds(8 * h, 8), :], buf.at[h], in_sems.at[h])
        for h in range(2)
    ]
    for copy in loads:
        copy.start()
    edges = fetch_all(
        [(f_ref.at[8], first.at[32]), (f_ref.at[9], last.at[32])], out_sems
    )
    wait_all(edges)
    stores = []
    for h, o_ref in ((0, lo_ref), (1, hi_ref)):
        loads[h].wait()
        for y in range(8):
            tiles = [buf[h, 8 * g : 8 * g + 8, y, :] for g in range(GROUPS)]
            wide = jnp.concatenate(tiles[:16], axis=0).T
            upper = jnp.concatenate(tiles[16:], axis=0)
            bands = jnp.concatenate([turn(upper, -32 * q, 1) for q in range(4)], axis=0)
            bands = bands.T[:32, :]
            out[h, y, :LANES, :] = wide
            out[h, y, LANES:, :] = bands
            first[8 * h + y] = wide[:8]
            last[8 * h + y] = wide[120:]
            first[16 + 8 * h + y] = bands[:8]
            last[16 + 8 * h + y] = bands[24:]
        dst = o_ref.at[:, pl.ds(0, NZ), :]
        copy = pltpu.make_async_copy(out.at[h], dst, out_sems.at[h])
        copy.start()
        stores.append(copy)
    for i, (a, b) in enumerate(((first, first_ref), (last, last_ref))):
        copy = pltpu.make_async_copy(a, b.at[pl.ds(0, 33)], out_sems.at[2 + i])
        copy.start()
        stores.append(copy)
    for copy in stores:
        copy.wait()


LOW = 192
HIGH = 208


def corners_kernel(
    lo_in, hi_in, f_hbm, w_hbm, x_hbm, lo_ref, hi_ref, fields, west, east, sems, out_sems
):
    del lo_in, hi_in
    loads = fetch_all([(w_hbm, west), (x_hbm, east), (f_hbm, fields)], sems)
    pairs = []
    for o_ref, base in ((lo_ref, 0), (hi_ref, 8)):
        for i, ref in enumerate((west, east)):
            for part in range(2):
                src = ref.at[pl.ds(16 * part + base, 8)]
                pairs.append((src, o_ref.at[:, pl.ds(160 + 16 * part + 8 * i, 8), :]))
    pairs.append((fields.at[pl.ds(0, 8)], hi_ref.at[:, pl.ds(192, 8), :]))
    pairs.append((west.at[32], hi_ref.at[0, pl.ds(200, 8), :]))
    pairs.append((east.at[32], hi_ref.at[1, pl.ds(200, 8), :]))
    wait_all(loads)
    wait_all(fetch_all(pairs, out_sems))


def edges_kernel(first_in, last_in, y_ref, first_ref, last_ref, sems):
    del first_in, last_in
    pairs = [(y_ref.at[8], first_ref.at[33]), (y_ref.at[9], last_ref.at[33])]
    wait_all(fetch_all(pairs, sems))


def moments_kernel(f_hbm, y_hbm, x_hbm, o_ref, f_ref, y_ref, x_ref, out, sems):
    pairs = [(f_hbm, f_ref), (y_hbm, y_ref), (x_hbm.at[pl.ds(32, 2)], x_ref)]
    wait_all(fetch_all(pairs, sems))
    lane8 = lane_ids((8, LANES))
    fields = []
    for f in range(4):
        main = jnp.concatenate([f_ref[2 * f], f_ref[2 * f + 1], y_ref[2 * f]], axis=0)
        extra = [
            turn(x_ref[0], -16 * (2 * f), 1),
            turn(x_ref[0], -16 * (2 * f + 1), 1),
            turn(x_ref[1], -16 * (2 * f), 1),
        ]
        extra = [jnp.where(lane8 < 16, x, 0.0) for x in extra]
        fields.append(jnp.concatenate([main, jnp.concatenate(extra, axis=0)], axis=1))
    shape = fields[0].shape
    lane, row = lane_ids(shape), row_ids(shape)
    last_x = jnp.where(lax.axis_index("gx") == 7, 127, -9)
    last_y = jnp.where(lax.axis_index("gy") == 15, 15, -9)
    keep_e = jnp.where(lane == last_x, 0.0, 1.0)
    keep_w = jnp.where(lane == last_x + 1, 0.0, 1.0)
    keep_n = jnp.where(row == last_y, 0.0, 1.0)
    keep_s = jnp.where(row == last_y + 1, 0.0, 1.0)
    apply = stencil(fields[2], fields[3], keep_e, keep_w, keep_n, keep_s)
    inside = (row >= 3) & (row < 19) & (lane >= 3) & (lane < 131)
    v0 = fields[:2]
    v1 = [apply(w) for w in v0]
    v2 = [apply(w) for w in v1]
    v3 = [apply(w) for w in v2]
    result = jnp.zeros((1, LANES), jnp.float32)
    pairs = ((v0, v0), (v0, v1), (v1, v1), (v1, v2), (v2, v2), (v2, v3))
    for j, (p, q) in enumerate(pairs):
        prod = jnp.where(inside, p[0] * q[0] + p[1] * q[1], 0.0)
        part = prod[:, :LANES] + prod[:, LANES:]
        total = jnp.sum(jnp.sum(part, axis=0, keepdims=True), axis=1, keepdims=True)
        result = jnp.where(lane_ids((1, LANES)) == j, total, result)
    out[...] = jnp.broadcast_to(result, (LANES, LANES))
    wait_all(fetch_all([(out, o_ref)], sems))


def basis_kernel(
    f_ref, w_ref, x_ref, s_ref, y_ref, o_hbm, t_hbm,
    own, west, east, south, s_w, s_e, north, o_ref, t_ref, sems,
):
    pairs = (
        (f_ref, own), (w_ref.at[pl.ds(32, 2)], west), (x_ref.at[pl.ds(32, 2)], east),
        (s_ref.at[:, pl.ds(192, 8), :], south), (s_ref.at[0, pl.ds(200, 8), :], s_w),
        (s_ref.at[1, pl.ds(200, 8), :], s_e), (y_ref, north),
    )
    wait_all(fetch_all(pairs, sems))
    lane8 = lane_ids((8, LANES))
    fields = []
    for f in range(4):
        main, extra = [], []
        for t in range(6):
            i = 2 * f + t % 2
            if t < 2:
                mid, left, right = south[i], s_w[...], s_e[...]
            elif t < 4:
                mid, left, right = own[i], west[0], east[0]
            else:
                mid, left, right = north[i], west[1], east[1]
            main.append(mid)
            right = turn(right, -16 * i, 1)
            left = turn(left, 112 - 16 * i, 1)
            extra.append(jnp.where(lane8 < 16, right, jnp.where(lane8 >= 112, left, 0.0)))
        fields.append(
            jnp.concatenate(
                [jnp.concatenate(main, axis=0), jnp.concatenate(extra, axis=0)], axis=1
            )
        )
    shape = fields[0].shape
    lane, row = lane_ids(shape), row_ids(shape)
    low_y = jnp.where(lax.axis_index("gy") == 0, 16, 0)
    high_y = jnp.where(lax.axis_index("gy") == 15, 32, 48)
    end_x = jnp.where(lax.axis_index("gx") == 7, 128, 144)
    start_x = jnp.where(lax.axis_index("gx") == 0, 256, 240)
    inside = (row >= low_y) & (row < high_y) & ((lane < end_x) | (lane >= start_x))
    inside = jnp.where(inside, 1.0, 0.0)
    fields = [x * inside for x in fields]
    apply = stencil(fields[2], fields[3], 1.0, 1.0, 1.0, 1.0)
    vectors = [fields[:2]]
    for _ in range(2):
        vectors.append([apply(w) * inside for w in vectors[-1]])
    fill = jnp.zeros((96, LANES), jnp.float32)
    for b in range(3):
        for c in range(2):
            v = vectors[b][c]
            o_ref[c, b] = v[16:32, :LANES]
            v = turn(v[8:40, :], 8, 1)
            t_ref[c, b, :LANES] = jnp.concatenate([v[:, :LANES], fill], axis=0).T
            t_ref[c, b, LANES:] = jnp.concatenate([v[:, LANES:], fill], axis=0).T[:16, :]
    wait_all(fetch_all([(o_ref, o_hbm), (t_ref, t_hbm)], sems))


def pivots_kernel(
    col_ref, lev_ref, basin_ref, owner_ref, geo_ref, drag_ref, surf_ref, melt_ref, mask_ref,
    inv_ref, plane_ref, inv, planes, basin, owner, mask, plane, sems, out_sems,
):
    pairs = [
        (col_ref, planes.at[4]), (basin_ref, basin), (owner_ref, owner), (mask_ref, mask),
        (geo_ref, planes.at[0]), (drag_ref, planes.at[1]), (surf_ref, planes.at[2]),
        (melt_ref, planes.at[3]),
    ]
    wait_all(fetch_all(pairs, sems))
    col = planes[4]

    def step(i, s):
        k = NZ - 1 - i
        lower = col * lev_ref[k - 1]
        one = 1.0 / (s + lower)
        inv[rows_at(k * ROWS, ROWS), :] = one
        return 1.0 + lower * (s * one)

    s = 1.0 + col * lev_ref[NZ - 1]
    stores = []
    for part, (a, b) in enumerate(((0, 80), (80, NZ - 1))):
        s = lax.fori_loop(a, b, step, s, unroll=16)
        if part == 1:
            inv[0:ROWS, :] = 1.0 / s
        at = pl.ds((1 - part) * 80 * ROWS, 80 * ROWS)
        stores.append(pltpu.make_async_copy(inv.at[at], inv_ref.at[at], out_sems.at[part]))
        stores[-1].start()
    for i in range(4):
        plane[16 * i : 16 * i + 16, :] = planes[i]
    plane[64:80, :] = jnp.where(mask[...] == 1, 1.0, 0.0)
    lane = lane_ids((1, LANES))
    slots = owner[...]
    ids = row_ids(slots.shape) * LANES + lane_ids(slots.shape)
    for j in range(4):
        mine = jnp.sum(jnp.where(lane == 32 * j, basin[0:1, :], 0), axis=1, keepdims=True)
        slot = jnp.where(ids == mine, slots, 0)
        slot = jnp.sum(jnp.sum(slot, axis=0, keepdims=True), axis=1, keepdims=True)
        slot = slot.astype(jnp.float32)
        plane[80 + 8 * j : 88 + 8 * j, :] = jnp.broadcast_to(slot, (8, LANES))
    plane[112:128, :] = col
    stores.append(pltpu.make_async_copy(plane, plane_ref, out_sems.at[2]))
    stores[-1].start()
    wait_all(stores)


def cg_coefficients(m):
    a0 = m[0] / m[1]
    rr1 = a0 * a0 * m[2] - m[0]
    b0 = rr1 / m[0]
    p1 = (1.0 + b0, -a0)
    q1 = p1[0] * p1[0] * m[1] + 2.0 * p1[0] * p1[1] * m[2] + p1[1] * p1[1] * m[3]
    a1 = rr1 / q1
    r2 = (1.0, -a0 - a1 * p1[0], -a1 * p1[1])

    def form(p, k):
        return (
            p[0] * p[0] * m[k]
            + 2.0 * p[0] * p[1] * m[k + 1]
            + (2.0 * p[0] * p[2] + p[1] * p[1]) * m[k + 2]
            + 2.0 * p[1] * p[2] * m[k + 3]
            + p[2] * p[2] * m[k + 4]
        )

    rr2 = form(r2, 0)
    b1 = rr2 / rr1
    p2 = (1.0 + b1 * p1[0], r2[1] + b1 * p1[1], r2[2])
    a2 = rr2 / form(p2, 1)
    inv = 1.0 / SCALE
    return (
        (a0 + a1 * p1[0] + a2 * p2[0]) * inv,
        (a1 * p1[1] + a2 * p2[1]) * inv,
        a2 * p2[2] * inv,
    )


def main_kernel(
    lo_ref, hi_ref, s_ref, n_ref, w_ref, x_ref,
    basis_ref, turned_ref, sums_ref, inv_ref, plane_ref, lev_ref,
    g_ref, vel_ref, send_ref,
    wide, band, wide_x, wide_y, band_x, band_y, flow, adv,
    west_b, east_b, basis, turned, sums, inv, plane, lev, solved, vel, send,
    sems, out_sems,
):
    lane8 = lane_ids((8, LANES))
    lane1 = lane_ids((1, LANES))
    copies = []

    def fetch(src, dst):
        copy = pltpu.make_async_copy(src, dst, sems.at[len(copies)])
        copy.start()
        copies.append(copy)
        return copy

    sums_here = fetch(sums_ref, sums)
    turned_here = fetch(turned_ref, turned)
    basis_here = fetch(basis_ref, basis)
    field_here = []
    for i, ref in enumerate((s_ref, lo_ref, hi_ref, n_ref)):
        y = pl.ds(8 * i, 8)
        field_here.append(fetch(ref.at[:, pl.ds(0, 128), :], wide.at[0, y, pl.ds(16, 128), :]))
        field_here.append(fetch(ref.at[:, pl.ds(128, 32), :], band.at[0, y, pl.ds(16, 32), :]))
    for at, x, ref in ((160, 8, w_ref), (168, 144, x_ref)):
        for y, msg in ((0, s_ref), (24, n_ref)):
            dst = wide.at[0, pl.ds(y, 8), pl.ds(x, 8), :]
            field_here.append(fetch(msg.at[:, pl.ds(at, 8), :], dst))
        dst = wide.at[0, pl.ds(8, 16), pl.ds(x, 8), :]
        field_here.append(fetch(ref.at[pl.ds(0, 16)], dst))
    for at, buf, ref in ((176, west_b, w_ref), (184, east_b, x_ref)):
        field_here.append(fetch(s_ref.at[:, pl.ds(at, 8), :], buf.at[pl.ds(0, 8)]))
        field_here.append(fetch(ref.at[pl.ds(16, 16)], buf.at[pl.ds(8, 16)]))
        field_here.append(fetch(n_ref.at[:, pl.ds(at, 8), :], buf.at[pl.ds(24, 8)]))
    later = [fetch(inv_ref, inv), fetch(lev_ref, lev), fetch(plane_ref, plane)]

    sums_here.wait()
    total = jnp.sum(sums[...], axis=0, keepdims=True)
    m = [
        jnp.sum(jnp.where(lane1 == j, total, 0.0), axis=1, keepdims=True) for j in range(6)
    ]
    c = cg_coefficients(m)

    def profile(k):
        height = (k.astype(jnp.float32) + 0.5) / NZ
        low = 1.0 - height
        low = low * low
        return 1.0 - low * low

    prof_w = profile(lane8)
    prof_b = profile(128 + lane8 % 32)
    turned_here.wait()

    def courants(i, carry):
        for j in range(6):
            at = rows_at((i * 6 + j) * 8, 8)
            for comp, o_ref in ((0, wide_x), (1, wide_y)):
                v = c[0] * turned[comp, 0, at, :]
                v = v + c[1] * turned[comp, 1, at, :]
                v = v + c[2] * turned[comp, 2, at, :]
                v = 3.0 * v
                for y in range(1, 31):
                    one = jnp.broadcast_to(v[:, y : y + 1], (8, LANES))
                    flow[comp, y, at, :] = one
                    o_ref[y, at, :] = 0.45 * jnp.tanh(one * prof_w)
        return carry

    lax.fori_loop(0, 3, courants, 0)

    def band_courants(i, carry):
        for j in range(3):
            t = i * 3 + j
            for comp, o_ref in ((0, band_x), (1, band_y)):
                for y in range(1, 31):
                    one = flow[comp, y, rows_at(t * 8, 8), :]
                    for q in range(1, 4):
                        other = flow[comp, y, rows_at(t * 8 + 32 * q, 8), :]
                        one = jnp.where(lane8 >= 32 * q, other, one)
                    o_ref[y, rows_at(t * 8, 8), :] = 0.45 * jnp.tanh(one * prof_b)
        return carry

    lax.fori_loop(0, 2, band_courants, 0)

    basis_here.wait()
    for comp in range(2):
        v = c[0] * basis[comp, 0] + c[1] * basis[comp, 1] + c[2] * basis[comp, 2]
        vel[comp] = v
    vel_out = pltpu.make_async_copy(vel, vel_ref, out_sems.at[0])
    vel_out.start()

    for copy in field_here:
        copy.wait()
    keep = jnp.where(lax.axis_index("gx") == 7, 0.0, 1.0)
    for y in range(32):
        wide[0, y, 144:152, :] = wide[0, y, 144:152, :] * keep
        left = turn(band[0, y, 40:48, :], 32, 1)
        left = jnp.where(lane8 < 32, turn(west_b[y], 32, 1), left)
        right = turn(band[0, y, 16:24, :], 96, 1)
        right = jnp.where(lane8 >= 96, turn(east_b[y] * keep, 96, 1), right)
        band[0, y, 8:16, :] = left
        band[0, y, 48:56, :] = right

    def substep(buf, cx_ref, cy_ref, s, t):
        src, dst = (s - 1) % 2, s % 2
        at = pl.multiple_of(t * 8, 8)
        mid = pl.ds(at + 8, 8)

        now = buf[src, s, mid, :]
        below = now - buf[src, s - 1, mid, :]
        for y in range(s, 32 - s):
            above = buf[src, y + 1, mid, :]
            west = buf[src, y, pl.ds(at + 7, 8), :]
            east = buf[src, y, pl.ds(at + 9, 8), :]
            cx = cx_ref[y, pl.ds(at, 8), :]
            cy = cy_ref[y, pl.ds(at, 8), :]
            rise = above - now
            across = jnp.where(cx > 0.0, now - west, east - now)
            along = jnp.where(cy > 0.0, below, rise)
            buf[dst, y, mid, :] = now - cx * across - cy * along
            now, below = above, rise

    for s in range(1, STEPS + 1):
        last = s == STEPS

        def tiles(i, carry, s=s, last=last):
            for j in range(8 if last else 6):
                t = i * 8 + j + 1 if last else i * 6 + j
                substep(wide, wide_x, wide_y, s, t)
            for j in range(2):
                substep(band, band_x, band_y, s, i * 2 + j + (1 if last else 0))
            return carry

        lax.fori_loop(0, 2 if last else 3, tiles, 0)

    def back(i, carry):
        for j in range(4):
            y = i * 4 + j
            x = wide[0, y + 8, 16:144, :].T
            for g in range(16):
                adv[pl.ds(g * 128 + y, 8, stride=16), :] = x[8 * g : 8 * g + 8, :]
        x = jnp.concatenate([band[0, i * 4 + j + 8, 16:48, :] for j in range(4)], axis=0).T
        for g in range(4):
            for j in range(4):
                out = None
                for q in range(4):
                    one = x[32 * q + 8 * g : 32 * q + 8 * g + 8, :]
                    one = turn(one, 32 * (q - j), 1)
                    out = one if q == 0 else jnp.where(lane8 >= 32 * q, one, out)
                adv[pl.ds((16 + g) * 128 + i * 4 + j, 8, stride=16), :] = out
        return carry

    lax.fori_loop(0, 4, back, 0)

    for copy in later:
        copy.wait()

    col = plane[112:128, :]

    def eliminate(i, above):
        k = NZ - 1 - i
        at = rows_at(k * ROWS, ROWS)
        one = inv[at, :]
        above = adv[at, :] * one + col * lev[k] * one * above
        solved[at, :] = above
        return above

    outs = [vel_out]
    parts = 5
    size = NZ // parts
    above = plane[32:48, :]
    for part in range(parts):
        above = lax.fori_loop(part * size, (part + 1) * size, eliminate, above, unroll=16)
        if part == parts - 1:
            u, v = vel[0], vel[1]
            bottom = plane[0:16, :] + 10.0 * plane[16:32, :] * (u * u + v * v)
            above = above + bottom * inv[0:ROWS, :]
            solved[0:ROWS, :] = above
        at = pl.ds((NZ - (part + 1) * size) * ROWS, size * ROWS)
        copy = pltpu.make_async_copy(solved.at[at], g_ref.at[at], out_sems.at[1 + part])
        copy.start()
        outs.append(copy)

    melt = jnp.where(plane[64:80, :] == 1.0, jnp.maximum(above - plane[48:64, :], 0.0), 0.0)
    melt = jnp.sum(melt, axis=0, keepdims=True) * MEAN
    place = row_ids((LANES, LANES)) * 2 + lane_ids((LANES, LANES))
    place = jnp.where(lane_ids((LANES, LANES)) < 2, place, -1).astype(jnp.float32)
    out = jnp.zeros((LANES, LANES), jnp.float32)
    for j in range(4):
        part = jnp.where((lane1 >= 32 * j) & (lane1 < 32 * j + 32), melt, 0.0)
        part = jnp.sum(part, axis=1, keepdims=True)
        slot = plane[80 + 8 * j : 81 + 8 * j, :]
        out = out + jnp.where(place == slot, part, 0.0)
    send[...] = out
    copy = pltpu.make_async_copy(send, send_ref, out_sems.at[1 + parts])
    copy.start()
    outs.append(copy)
    for copy in outs:
        copy.wait()


def back_kernel(g_ref, inv_ref, e_ref, mask_ref, plane_ref, lev_ref, o_ref):
    col = plane_ref[112:128, :]
    ice = mask_ref[...] == 1

    def step(k, below):
        at = rows_at(k * ROWS, ROWS)
        below = g_ref[at, :] + col * lev_ref[k - 1] * inv_ref[at, :] * below
        o_ref[at, :] = jnp.where(ice, below, e_ref[at, :])
        return below

    below = g_ref[0:ROWS, :]
    o_ref[0:ROWS, :] = jnp.where(ice, below, e_ref[0:ROWS, :])
    lax.fori_loop(1, NZ, step, below, unroll=16)


MEAN = 256 / 262144


def per_device(
    enthalpy,
    conduct_col,
    conduct_level,
    surface_enthalpy,
    geothermal,
    melt_level,
    viscosity,
    drag,
    driving_stress,
    ice_mask,
    basin,
    owner_slot,
):
    nx, ny = lax.axis_size("gx"), lax.axis_size("gy")
    both = ("gx", "gy")
    up_x = [(i, i + 1) for i in range(nx - 1)]
    ring_x = [((i + 1) % nx, i) for i in range(nx)]
    up_y = [(i, i + 1) for i in range(ny - 1)]
    down_y = [(i + 1, i) for i in range(ny - 1)]
    ring_y = [((i + 1) % ny, i) for i in range(ny)]
    dma = pltpu.SemaphoreType.DMA

    def vmem(*shape, dtype=jnp.float32):
        return pltpu.VMEM(shape, dtype)

    tie = lax.optimization_barrier

    with jax.named_scope("fields"):
        (fields,) = call(
            fields_kernel, [f32(10, 8, LANES)], driving_stress, viscosity, drag,
            places="aaa" + "a",
            scratch=(vmem(4, ROWS, LANES), vmem(10, 8, LANES), dma((3,))),
            limit=FULL,
        )
        rows = lax.ppermute(fields, "gy", ring_y)
    with jax.named_scope("levels_on_lanes"):
        low, high, first, last = call(
            transpose_kernel,
            [f32(8, LOW, LANES), f32(8, HIGH, LANES)] + [f32(34, 8, LANES)] * 2,
            enthalpy, fields, places="aa" + "aaaa",
            scratch=(
                vmem(2, NZ, 8, LANES), vmem(2, 8, NZ, LANES),
                vmem(33, 8, LANES), vmem(33, 8, LANES), dma((2,)), dma((4,)),
            ),
            limit=FULL,
        )
        first, last = call(
            edges_kernel, [f32(34, 8, LANES)] * 2, first, last, rows, places="aaa" + "aa",
            scratch=(dma((2,)),), limit=FULL, aliases={0: 0, 1: 1},
        )
    with jax.named_scope("moments"):
        east = lax.ppermute(first, "gx", ring_x)
        west = lax.ppermute(last, "gx", up_x)
        (sums,) = call(
            moments_kernel, [f32(LANES, LANES)], fields, rows, east, places="aaa" + "a",
            scratch=(
                vmem(10, 8, LANES), vmem(10, 8, LANES), vmem(2, 8, LANES),
                vmem(LANES, LANES), dma((3,)),
            ),
            limit=FULL,
        )

    with jax.named_scope("halo"):
        low, high = call(
            corners_kernel, [f32(8, LOW, LANES), f32(8, HIGH, LANES)],
            low, high, fields, west, east, places="aaaaa" + "aa",
            scratch=(
                vmem(10, 8, LANES), vmem(34, 8, LANES), vmem(34, 8, LANES), dma((3,)), dma((11,)),
            ),
            limit=FULL, aliases={0: 0, 1: 1},
        )
        south = lax.ppermute(high, "gy", up_y)
        north = lax.ppermute(low, "gy", down_y)

    with jax.named_scope("moments"):
        every = lax.all_to_all(sums.reshape(LANES, 1, LANES), both, 0, 0)
        every = every.reshape(LANES, LANES)

    with jax.named_scope("prepare"):
        late_col, _ = tie((conduct_col, sums))
        inv, plane = call(
            pivots_kernel,
            [f32(NZ * ROWS, LANES), f32(LANES, LANES)],
            late_col, conduct_level, basin, owner_slot.reshape(2, LANES),
            geothermal, drag, surface_enthalpy, melt_level, ice_mask,
            places="asaaaaaaa" + "aa",
            scratch=(
                vmem(NZ * ROWS, LANES), vmem(5, ROWS, LANES),
                vmem(ROWS, LANES, dtype=jnp.int32), vmem(2, LANES, dtype=jnp.int32),
                vmem(ROWS, LANES, dtype=jnp.int32), vmem(LANES, LANES), dma((8,)), dma((3,)),
            ),
            limit=FULL,
        )
        basis, turned = call(
            basis_kernel, [f32(2, 3, ROWS, LANES), f32(2, 3, WIDE, LANES)],
            fields, west, east, south, rows, places="aaaaa" + "aa",
            scratch=(
                vmem(10, 8, LANES), vmem(2, 8, LANES), vmem(2, 8, LANES), vmem(8, 8, LANES),
                vmem(8, LANES), vmem(8, LANES), vmem(10, 8, LANES),
                vmem(2, 3, ROWS, LANES), vmem(2, 3, WIDE, LANES), dma((7,)),
            ),
            limit=FULL,
        )

    with jax.named_scope("transport"):
        reduced, velocity, send = call(
            main_kernel,
            [f32(NZ * ROWS, LANES), f32(2, ROWS, LANES), f32(LANES, LANES)],
            low, high, south, north, west, east,
            basis, turned, every, inv, plane, conduct_level,
            places="a" * 12 + "aaa",
            scratch=(
                vmem(2, 32, WIDE + 16, LANES), vmem(2, 32, BAND + 16, LANES),
                vmem(32, WIDE, LANES), vmem(32, WIDE, LANES),
                vmem(32, BAND, LANES), vmem(32, BAND, LANES),
                vmem(2, 32, WIDE, LANES), vmem(NZ * ROWS, LANES),
                vmem(32, 8, LANES), vmem(32, 8, LANES),
                vmem(2, 3, ROWS, LANES), vmem(2, 3, WIDE, LANES), vmem(LANES, LANES),
                vmem(NZ * ROWS, LANES), vmem(LANES, LANES), pltpu.SMEM((NZ,), jnp.float32),
                vmem(NZ * ROWS, LANES), vmem(2, ROWS, LANES), vmem(LANES, LANES),
                dma((26,)), dma((7,)),
            ),
            limit=FULL,
        )

    with jax.named_scope("basin_melt"):
        received = lax.all_to_all(send.reshape(LANES, 1, LANES), both, 0, 0)
        basin_melt = jnp.sum(received.reshape(LANES, LANES)[:, :2], axis=0)

    with jax.named_scope("substitution"):
        (solved,) = call(
            back_kernel, [f32(NZ * ROWS, LANES)],
            reduced, inv, enthalpy.reshape(NZ * ROWS, LANES), ice_mask, plane, conduct_level,
            places="vvvvvs" + "d",
        )
    return (solved.reshape(NZ, ROWS, LANES), velocity, basin_melt)


def solution(mesh):
    return jax.shard_map(
        per_device,
        mesh=mesh,
        in_specs=(
            P(None, "gy", "gx"),
            P("gy", "gx"),
            P(),
            P("gy", "gx"),
            P("gy", "gx"),
            P("gy", "gx"),
            P("gy", "gx"),
            P("gy", "gx"),
            P(None, "gy", "gx"),
            P("gy", "gx"),
            P("gy", "gx"),
            P(),
        ),
        out_specs=(P(None, "gy", "gx"), P(None, "gy", "gx"), P(("gx", "gy"))),
        check_vma=False,
    )
```

profile of v0, /device:TPU:1, one launch (start us, length us, event | category | flops | bytes accessed | tf_op | source)
XLA Modules:
  0.0 84.3 jit_solution(3929933567438108451)
XLA Ops:
  0.6 1.4 %fields.1.f_ref.f_hbm = f32[10,8,128]{2,1,0:T(8,128)} custom-call(f32[2,16,128]{2,1,0:T(8,128)} %stress_ref.1, f32[16,128]{1,0:T(8,128)} %visc_ref.1, f32[16,128]{1,0:T(8,128)} %drag_ref.3), custom_call_target="tpu_custom_call" | custom-call | bytes 73728 | tf_op jit(solution)/shard_map/fields/pallas_call | solution.py:43
  2.1 7.1 %collective-permute-start = (f32[10,8,128]{2,1,0:T(8,128)}, f32[10,8,128]{2,1,0:T(8,128)S(1)}, u32[]{:S(2)}, u32[]{:S(2)}) collective-permute-start(f32[10,8,128]{2,1,0:T(8,128)} %fields.1.f_ref.f_hbm), channel_id=1, source_target_pairs={{1,0},{2,1},{3,2},{4,3},{5,4},{6,5},{7,6},{8,7},{9,8},{10,9},{11,1... | collective-permute-start | bytes 122888 | tf_op jit(solution)/shard_map/fields/ppermute | solution.py:618
  9.2 3.0 %levels_on_lanes.2 = (f32[8,192,128]{2,1,0:T(8,128)}, f32[8,208,128]{2,1,0:T(8,128)}, f32[34,8,128]{2,1,0:T(8,128)}, f32[34,8,128]{2,1,0:T(8,128)}) custom-call(f32[160,16,128]{2,1,0:T(8,128)} %e_ref.1, f32[10,8,128]{2,1,0:T(8,128)} %fields.1.f_ref.f_hbm), custom_call_target="tpu_custom_call" | custom-call | bytes 3268608 | tf_op jit(solution)/shard_map/levels_on_lanes/pallas_call | solution.py:43
  12.2 0.0 collective-permute-done.y_ref.y_hbm
  12.2 0.0 copy-start.10
  12.3 0.6 copy-done.10
  12.9 1.4 %levels_on_lanes.3 = (f32[34,8,128]{2,1,0:T(8,128)}, f32[34,8,128]{2,1,0:T(8,128)}) custom-call(f32[34,8,128]{2,1,0:T(8,128)} %get-tuple-element.21.first_in, f32[34,8,128]{2,1,0:T(8,128)} %get-tuple-element.22.last_in, f32[10,8,128]{2,1,0:T(8,128)} %copy-done.10), custom_call_target="tpu_custom_call", output_to_operand_aliasing={{0}: (0, {}), {1}: (1, {})} | custom-call | bytes 598016 | tf_op jit(solution)/shard_map/levels_on_lanes/pallas_call | solution.py:43
  14.2 4.0 %collective-permute-start.1 = (f32[34,8,128]{2,1,0:T(8,128)}, f32[34,8,128]{2,1,0:T(8,128)S(1)}, u32[]{:S(2)}, u32[]{:S(2)}) collective-permute-start(f32[34,8,128]{2,1,0:T(8,128)} %get-tuple-element.23), channel_id=1, source_target_pairs={{0,16},{16,32},{32,48},{48,64},{64,80},{80,96},{96,112},{1,17},{17... | collective-permute-start | bytes 417800 | tf_op jit(solution)/shard_map/moments/ppermute | solution.py:636
  18.2 0.0 collective-permute-start.2
  18.2 2.3 %collective-permute-done.1.w_hbm.w_ref = f32[34,8,128]{2,1,0:T(8,128)S(1)} collective-permute-done((f32[34,8,128]{2,1,0:T(8,128)}, f32[34,8,128]{2,1,0:T(8,128)S(1)}, u32[]{:S(2)}, u32[]{:S(2)}) %collective-permute-start.1) | collective-permute-done | bytes 139296 | tf_op jit(solution)/shard_map/moments/ppermute | solution.py:636
  20.5 0.0 copy-start.8
  20.5 2.4 %collective-permute-done.2.x_hbm.x_ref = f32[34,8,128]{2,1,0:T(8,128)S(1)} collective-permute-done((f32[34,8,128]{2,1,0:T(8,128)}, f32[34,8,128]{2,1,0:T(8,128)S(1)}, u32[]{:S(2)}, u32[]{:S(2)}) %collective-permute-start.2) | collective-permute-done | bytes 139296 | tf_op jit(solution)/shard_map/moments/ppermute | solution.py:635
  22.9 0.0 copy-start.7
  22.9 0.0 copy-done.8
  22.9 0.7 copy-done.7
  23.6 1.9 %halo.1 = (f32[8,192,128]{2,1,0:T(8,128)}, f32[8,208,128]{2,1,0:T(8,128)}) custom-call(f32[8,192,128]{2,1,0:T(8,128)} %get-tuple-element.19.lo_in, f32[8,208,128]{2,1,0:T(8,128)} %get-tuple-element.20.hi_in, f32[10,8,128]{2,1,0:T(8,128)} %fields.1.f_ref.f_hbm, f32[34,8,128]{2,1,0:T(8,128)} %copy-done.8, ...), custom_call_target="tpu_custom_call", output_to_operand_aliasing={{0}: (0, {}), {1}: (1, {})} | custom-call | bytes 3596288 | tf_op jit(solution)/shard_map/halo/pallas_call | solution.py:43
  25.4 1.3 %collective-permute-start.3 = (f32[8,208,128]{2,1,0:T(8,128)}, f32[8,208,128]{2,1,0:T(8,128)S(1)}, u32[]{:S(2)}, u32[]{:S(2)}) collective-permute-start(f32[8,208,128]{2,1,0:T(8,128)} %get-tuple-element.26.hi_ref), channel_id=1, source_target_pairs={{0,1},{1,2},{2,3},{3,4},{4,5},{5,6},{6,7},{7,8},{8,9},{9,10},{10,1... | collective-permute-start | bytes 2555912 | tf_op jit(solution)/shard_map/halo/ppermute | solution.py:655
  26.8 1.3 %collective-permute-start.4 = (f32[8,192,128]{2,1,0:T(8,128)}, f32[8,192,128]{2,1,0:T(8,128)S(1)}, u32[]{:S(2)}, u32[]{:S(2)}) collective-permute-start(f32[8,192,128]{2,1,0:T(8,128)} %get-tuple-element.25.lo_ref), channel_id=1, source_target_pairs={{1,0},{2,1},{3,2},{4,3},{5,4},{6,5},{7,6},{8,7},{9,8},{10,9},{11,1... | collective-permute-start | bytes 2359304 | tf_op jit(solution)/shard_map/halo/ppermute | solution.py:656
  28.1 1.9 %moments.1 = f32[128,128]{1,0:T(8,128)} custom-call(f32[10,8,128]{2,1,0:T(8,128)} %fields.1.f_ref.f_hbm, f32[10,8,128]{2,1,0:T(8,128)} %copy-done.10, f32[34,8,128]{2,1,0:T(8,128)} %copy-done.7), custom_call_target="tpu_custom_call" | custom-call | bytes 286720 | tf_op jit(solution)/shard_map/moments/pallas_call | solution.py:43
  30.0 10.3 %all-to-all-start = ((f32[128,1,128]{2,1,0:T(1,128)}), f32[128,1,128]{2,1,0:T(1,128)S(1)}, u32[]{:S(2)}, u32[]{:S(2)}) async-start(f32[128,1,128]{2,1,0:T(1,128)} %bitcast.15), calls=%async_computation | async-start | bytes 131072 | tf_op jit(solution)/shard_map/moments/all_to_all | solution.py:659
  40.3 4.2 %prepare.3 = (f32[2560,128]{1,0:T(8,128)}, f32[128,128]{1,0:T(8,128)}) custom-call(f32[16,128]{1,0:T(8,128)} %col_ref, f32[160]{0:T(256)} %lev_ref.5, s32[16,128]{1,0:T(8,128)} %basin_ref.1, s32[2,128]{1,0:T(2,128)} %bitcast.17, f32[16,128]{1,0:T(8,128)} %geo_ref.1, f32[16,128]{1,0:T(8,128)} %drag_ref.3, f32[16,128]{1,0:T(8,128)} %surf_ref.1, ...), custom_call_target="tpu_custom_call" | custom-call | bytes 1435264 | tf_op jit(solution)/shard_map/prepare/pallas_call | solution.py:43
  44.5 0.5 collective-permute-done.3.s_ref
  45.0 0.0 copy-start.6
  45.0 0.9 %copy-done.6 = f32[8,208,128]{2,1,0:T(8,128)} copy-done((f32[8,208,128]{2,1,0:T(8,128)}, f32[8,208,128]{2,1,0:T(8,128)S(1)}, u32[]{:S(2)}) %copy-start.6) | copy-done | bytes 851992
  45.9 2.2 %prepare.2 = (f32[2,3,16,128]{3,2,1,0:T(8,128)}, f32[2,3,144,128]{3,2,1,0:T(8,128)}) custom-call(f32[10,8,128]{2,1,0:T(8,128)} %fields.1.f_ref.f_hbm, f32[34,8,128]{2,1,0:T(8,128)} %copy-done.8, f32[34,8,128]{2,1,0:T(8,128)} %copy-done.7, f32[8,208,128]{2,1,0:T(8,128)} %copy-done.6, f32[10,8,128]{2,1,0:T(8,128)} %copy-done.10), custom_call_target="tpu_custom_call" | custom-call | bytes 1703936 | tf_op jit(solution)/shard_map/prepare/pallas_call | solution.py:43
  48.1 2.6 %all-to-all-done = f32[128,1,128]{2,1,0:T(1,128)S(1)} async-done(((f32[128,1,128]{2,1,0:T(1,128)}), f32[128,1,128]{2,1,0:T(1,128)S(1)}, u32[]{:S(2)}, u32[]{:S(2)}) %all-to-all-start) | async-done | bytes 65568 | tf_op jit(solution)/shard_map/moments/all_to_all | solution.py:659
  50.8 0.0 copy-start.11
  50.8 0.0 collective-permute-done.4.n_ref
  50.8 0.0 copy-start.9
  50.8 0.6 copy-done.11
  51.4 0.3 copy-done.9
  51.7 0.0 copy-start
  51.7 0.0 copy-start.1
  51.7 0.0 copy-start.3
  51.7 0.0 copy-start.4
  51.7 0.0 copy-start.5
  51.7 13.4 %transport.1 = (f32[2560,128]{1,0:T(8,128)}, f32[2,16,128]{2,1,0:T(8,128)}, f32[128,128]{1,0:T(8,128)}) custom-call(f32[8,192,128]{2,1,0:T(8,128)} %get-tuple-element.25.lo_ref, f32[8,208,128]{2,1,0:T(8,128)} %get-tuple-element.26.hi_ref, f32[8,208,128]{2,1,0:T(8,128)} %copy-done.6, f32[8,192,128]{2,1,0:T(8,128)} %copy-done.9, f32[34,8,128]{2,1,0:T(8,128)} %copy-done.8, ...), custom_call_target="tpu_custom_call" | custom-call | bytes 6881920 | tf_op jit(solution)/shard_map/transport/pallas_call | solution.py:43
  65.2 8.8 %all-to-all-start.1 = ((f32[128,1,128]{2,1,0:T(1,128)}), f32[128,1,128]{2,1,0:T(1,128)S(1)}, u32[]{:S(2)}, u32[]{:S(2)}) async-start(f32[128,1,128]{2,1,0:T(1,128)} %bitcast.16), calls=%async_computation.1 | async-start | bytes 131072 | tf_op jit(solution)/shard_map/basin_melt/all_to_all | solution.py:710
  73.9 0.0 copy-done
  74.0 0.0 copy-done.1
  74.0 0.0 copy-done.3
  74.0 0.0 copy-done.4
  74.0 0.0 copy-done.5
  74.0 0.0 copy-start.2
  74.0 1.3 %copy-done.2 = f32[2560,128]{1,0:T(8,128)S(1)} copy-done((f32[2560,128]{1,0:T(8,128)S(1)}, f32[2560,128]{1,0:T(8,128)}, u32[]{:S(2)}) %copy-start.2) | copy-done | bytes 1310744
  75.3 2.1 %substitution.1 = f32[2560,128]{1,0:T(8,128)} custom-call(f32[2560,128]{1,0:T(8,128)S(1)} %copy-done.2, f32[2560,128]{1,0:T(8,128)S(1)} %copy-done.1, f32[2560,128]{1,0:T(8,128)S(1)} %bitcast.11, s32[16,128]{1,0:T(8,128)S(1)} %copy-done.4, f32[128,128]{1,0:T(8,128)S(1)} %copy-done.3, f32[160]{0:T(256)S(1)} %copy-done.5), custom_call_target="tpu_custom_call" | custom-call | bytes 5317248 | tf_op jit(solution)/shard_map/substitution/pallas_call | solution.py:43
  77.4 6.3 %all-to-all-done.1 = f32[128,1,128]{2,1,0:T(1,128)S(1)} async-done(((f32[128,1,128]{2,1,0:T(1,128)}), f32[128,1,128]{2,1,0:T(1,128)S(1)}, u32[]{:S(2)}, u32[]{:S(2)}) %all-to-all-start.1) | async-done | bytes 65568 | tf_op jit(solution)/shard_map/basin_melt/all_to_all | solution.py:710
  83.7 0.5 slice_reduce_fusion
Async XLA Ops:
  2.1 10.2 %collective-permute-start = (f32[10,8,128]{2,1,0:T(8,128)}, f32[10,8,128]{2,1,0:T(8,128)S(1)}, u32[]{:S(2)}, u32[]{:S(2)}) collective-permute-start(f32[10,8,128]{2,1,0:T(8,128)} %fields.1.f_ref.f_hbm), channel_id=1, source_target_pairs={{1,0},{2,1},{3,2},{4,3},{5,4},{6,5},{7,6},{8,7},{9,8},{10,9},{11,1... | collective-permute-start | bytes 122888 | tf_op jit(solution)/shard_map/fields/ppermute | solution.py:618
  12.2 0.6 copy-start.10
  14.2 6.3 %collective-permute-start.1 = (f32[34,8,128]{2,1,0:T(8,128)}, f32[34,8,128]{2,1,0:T(8,128)S(1)}, u32[]{:S(2)}, u32[]{:S(2)}) collective-permute-start(f32[34,8,128]{2,1,0:T(8,128)} %get-tuple-element.23), channel_id=1, source_target_pairs={{0,16},{16,32},{32,48},{48,64},{64,80},{80,96},{96,112},{1,17},{17... | collective-permute-start | bytes 417800 | tf_op jit(solution)/shard_map/moments/ppermute | solution.py:636
  18.2 4.7 %collective-permute-start.2 = (f32[34,8,128]{2,1,0:T(8,128)}, f32[34,8,128]{2,1,0:T(8,128)S(1)}, u32[]{:S(2)}, u32[]{:S(2)}) collective-permute-start(f32[34,8,128]{2,1,0:T(8,128)} %get-tuple-element.24), channel_id=1, source_target_pairs={{16,0},{32,16},{48,32},{64,48},{80,64},{96,80},{112,96},{0,112},{1... | collective-permute-start | bytes 417800 | tf_op jit(solution)/shard_map/moments/ppermute | solution.py:635
  20.5 2.4 %copy-start.8 = (f32[34,8,128]{2,1,0:T(8,128)}, f32[34,8,128]{2,1,0:T(8,128)S(1)}, u32[]{:S(2)}) copy-start(f32[34,8,128]{2,1,0:T(8,128)S(1)} %collective-permute-done.1.w_hbm.w_ref) | copy-start | bytes 417796
  22.9 0.7 copy-start.7
  25.4 19.6 %collective-permute-start.3 = (f32[8,208,128]{2,1,0:T(8,128)}, f32[8,208,128]{2,1,0:T(8,128)S(1)}, u32[]{:S(2)}, u32[]{:S(2)}) collective-permute-start(f32[8,208,128]{2,1,0:T(8,128)} %get-tuple-element.26.hi_ref), channel_id=1, source_target_pairs={{0,1},{1,2},{2,3},{3,4},{4,5},{5,6},{6,7},{7,8},{8,9},{9,10},{10,1... | collective-permute-start | bytes 2555912 | tf_op jit(solution)/shard_map/halo/ppermute | solution.py:655
  26.8 24.0 %collective-permute-start.4 = (f32[8,192,128]{2,1,0:T(8,128)}, f32[8,192,128]{2,1,0:T(8,128)S(1)}, u32[]{:S(2)}, u32[]{:S(2)}) collective-permute-start(f32[8,192,128]{2,1,0:T(8,128)} %get-tuple-element.25.lo_ref), channel_id=1, source_target_pairs={{1,0},{2,1},{3,2},{4,3},{5,4},{6,5},{7,6},{8,7},{9,8},{10,9},{11,1... | collective-permute-start | bytes 2359304 | tf_op jit(solution)/shard_map/halo/ppermute | solution.py:656
  30.0 20.8 %all-to-all-start = ((f32[128,1,128]{2,1,0:T(1,128)}), f32[128,1,128]{2,1,0:T(1,128)S(1)}, u32[]{:S(2)}, u32[]{:S(2)}) async-start(f32[128,1,128]{2,1,0:T(1,128)} %bitcast.15), calls=%async_computation | async-start | bytes 131072 | tf_op jit(solution)/shard_map/moments/all_to_all | solution.py:659
  45.0 0.9 %copy-start.6 = (f32[8,208,128]{2,1,0:T(8,128)}, f32[8,208,128]{2,1,0:T(8,128)S(1)}, u32[]{:S(2)}) copy-start(f32[8,208,128]{2,1,0:T(8,128)S(1)} %collective-permute-done.3.s_ref) | copy-start | bytes 2555908
  50.8 0.6 copy-start.11
  50.8 0.9 %copy-start.9 = (f32[8,192,128]{2,1,0:T(8,128)}, f32[8,192,128]{2,1,0:T(8,128)S(1)}, u32[]{:S(2)}) copy-start(f32[8,192,128]{2,1,0:T(8,128)S(1)} %collective-permute-done.4.n_ref) | copy-start | bytes 2359300
  51.7 22.2 %copy-start = (f32[160,16,128]{2,1,0:T(8,128)S(1)}, f32[160,16,128]{2,1,0:T(8,128)}, u32[]{:S(2)}) copy-start(f32[160,16,128]{2,1,0:T(8,128)} %e_ref.1) | copy-start | bytes 3932164
  51.7 22.2 %copy-start.1 = (f32[2560,128]{1,0:T(8,128)S(1)}, f32[2560,128]{1,0:T(8,128)}, u32[]{:S(2)}) copy-start(f32[2560,128]{1,0:T(8,128)} %get-tuple-element.30.inv_ref) | copy-start | bytes 3932164
  51.7 22.2 %copy-start.3 = (f32[128,128]{1,0:T(8,128)S(1)}, f32[128,128]{1,0:T(8,128)}, u32[]{:S(2)}) copy-start(f32[128,128]{1,0:T(8,128)} %get-tuple-element.31.plane_ref) | copy-start | bytes 196612
  51.7 22.3 %copy-start.4 = (s32[16,128]{1,0:T(8,128)S(1)}, s32[16,128]{1,0:T(8,128)}, u32[]{:S(2)}) copy-start(s32[16,128]{1,0:T(8,128)} %mask_ref.3) | copy-start | bytes 24580
  51.7 22.3 %copy-start.5 = (f32[160]{0:T(256)S(1)}, f32[160]{0:T(256)}, u32[]{:S(2)}) copy-start(f32[160]{0:T(256)} %lev_ref.5) | copy-start | bytes 1924
  65.2 18.6 %all-to-all-start.1 = ((f32[128,1,128]{2,1,0:T(1,128)}), f32[128,1,128]{2,1,0:T(1,128)S(1)}, u32[]{:S(2)}, u32[]{:S(2)}) async-start(f32[128,1,128]{2,1,0:T(1,128)} %bitcast.16), calls=%async_computation.1 | async-start | bytes 131072 | tf_op jit(solution)/shard_map/basin_melt/all_to_all | solution.py:710
  74.0 1.3 %copy-start.2 = (f32[2560,128]{1,0:T(8,128)S(1)}, f32[2560,128]{1,0:T(8,128)}, u32[]{:S(2)}) copy-start(f32[2560,128]{1,0:T(8,128)} %get-tuple-element.32.g_ref) | copy-start | bytes 3932164
where the time goes:
time: 84.9 us; the launch traced here: 84.3 us
  starting transfers between devices  32.8 us (39%)
  Pallas kernels  31.6 us (37%)
  waiting for transfers between devices  14.1 us (17%)
  local copies, waits for them, and re-layouts  4.42 us (5%)
    pallas_call x9, Pallas kernels, call(): pl.pallas_call(kernel, out_shape=outs, in_specs=specs[:len(args)], out_sp...  31.6 us
    all_to_all x1, starting transfers between devices, per_device(): every = lax.all_to_all(sums.reshape(LANES, 1, LANES), both, 0, 0)  10.3 us
    all_to_all x1, starting transfers between devices, per_device(): received = lax.all_to_all(send.reshape(LANES, 1, LANES), both, 0, 0)  8.78 us
    ppermute x1, starting transfers between devices, per_device(): rows = lax.ppermute(fields, 'gy', ring_y)  7.11 us
    all_to_all x1, waiting for transfers between devices, per_device(): received = lax.all_to_all(send.reshape(LANES, 1, LANES), both, 0, 0)  6.31 us
    unnamed x24, local copies, waits for them, and re-layouts  4.42 us
    ppermute x1, starting transfers between devices, per_device(): west = lax.ppermute(last, 'gx', up_x)  3.96 us
    all_to_all x1, waiting for transfers between devices, per_device(): every = lax.all_to_all(sums.reshape(LANES, 1, LANES), both, 0, 0)  2.64 us
  transfers between devices with their start and end apart: 7, of which 5 were waited for; matrix products, arithmetic and copies ran while one was open for 0% of the time, Pallas kernels for 16%

commit v1 on v0

v1 whole, which is shorter than its diff:
```python
import jax
import jax.numpy as jnp
from jax import lax
from jax.experimental import pallas as pl
from jax.experimental.pallas import tpu as pltpu
from jax.sharding import PartitionSpec as P

STEPS = 8
NZ = 160
ROWS = 16
LANES = 128
GROUPS = NZ // 8
SCALE = 16.0
WIDE = 144
BAND = 48
FULL = 63.4
MOST = 60
SMALL = 8
COPIES = 4


def lane_ids(shape):
    return lax.broadcasted_iota(jnp.int32, shape, len(shape) - 1)


def row_ids(shape):
    return lax.broadcasted_iota(jnp.int32, shape, len(shape) - 2)


def turn(x, shift, axis):
    shift = shift % x.shape[axis]
    return x if shift == 0 else pltpu.roll(x, shift, axis)


def f32(*shape):
    return jax.ShapeDtypeStruct(shape, jnp.float32)


def call(kernel, outs, *args, places, scratch=(), limit=8, cost=None, aliases={}):
    spaces = {"v": pltpu.VMEM, "s": pltpu.SMEM, "a": pltpu.HBM}
    specs = [
        pl.BlockSpec(memory_space=spaces[p]) if p in spaces else pl.BlockSpec()
        for p in places
    ]
    if cost is None:
        cost = sum(a.size * 4 for a in args) + sum(o.size * 4 for o in outs)
    return pl.pallas_call(
        kernel,
        out_shape=outs,
        in_specs=specs[: len(args)],
        out_specs=specs[len(args) :],
        scratch_shapes=list(scratch),
        input_output_aliases=aliases,
        compiler_params=pltpu.CompilerParams(vmem_limit_bytes=int(limit * 1024 * 1024)),
        cost_estimate=pl.CostEstimate(
            flops=0, bytes_accessed=cost, transcendentals=0
        ),
    )(*args)


def rows_at(start, size):
    return pl.ds(pl.multiple_of(start, size if size in (8, 16) else 8), size)


def stencil(visc, drag, keep_e, keep_w, keep_n, keep_s):
    wide = visc.shape[1]
    tall = visc.shape[0]
    east = 0.5 * (visc + turn(visc, -1, 1) * keep_e)
    west = 0.5 * (visc + turn(visc, 1, 1) * keep_w)
    north = 0.5 * (visc + turn(visc, -1, 0) * keep_n)
    south = 0.5 * (visc + turn(visc, 1, 0) * keep_s)
    center = drag + east + west + north + south
    inv = 1.0 / SCALE
    center, east, west, north, south = (
        center * inv,
        east * keep_e * inv,
        west * keep_w * inv,
        north * keep_n * inv,
        south * keep_s * inv,
    )

    def apply(w):
        return (
            center * w
            - east * turn(w, -1, 1)
            - west * turn(w, 1, 1)
            - north * turn(w, -1, 0)
            - south * turn(w, 1, 0)
        )

    return apply


def edge_tile(tiles, first):
    lane = lane_ids((8, LANES))
    out = jnp.zeros((8, LANES), jnp.float32)
    for i in range(8):
        x = turn(tiles[i], 16 * i if first else 16 * i - 112, 1)
        out = jnp.where((lane >= 16 * i) & (lane < 16 * i + 16), x, out)
    return out


def fetch_all(pairs, sems):
    copies = [
        pltpu.make_async_copy(src, dst, sems.at[i]) for i, (src, dst) in enumerate(pairs)
    ]
    for copy in copies:
        copy.start()
    return copies


def wait_all(copies):
    for copy in copies:
        copy.wait()


def fields_kernel(stress_ref, visc_ref, drag_ref, f_ref, raw, out, sems):
    pairs = [(stress_ref, raw.at[pl.ds(0, 2)]), (visc_ref, raw.at[2]), (drag_ref, raw.at[3])]
    wait_all(fetch_all(pairs, sems))
    tiles = [raw[i // 2, 8 * (i % 2) : 8 * (i % 2) + 8, :] for i in range(8)]
    for i in range(8):
        out[i] = tiles[i]
    out[8] = edge_tile(tiles, True)
    out[9] = edge_tile(tiles, False)
    wait_all(fetch_all([(out, f_ref)], sems))


LOW = 160
HIGH = 168


def transpose_kernel(
    e_ref, f_ref, lo_ref, hi_ref, first_ref, last_ref,
    buf, out, fields, first, last, in_sems, out_sems,
):
    loads = fetch_all(
        [(e_ref.at[:, pl.ds(8 * h, 8), :], buf.at[h]) for h in range(2)]
        + [(f_ref.at[pl.ds(0, 8)], fields)],
        in_sems,
    )
    stores = []

    def send(src, dst):
        copy = pltpu.make_async_copy(src, dst, out_sems.at[len(stores)])
        copy.start()
        stores.append(copy)

    for h, o_ref in ((0, lo_ref), (1, hi_ref)):
        loads[h].wait()
        for y in range(8):
            tiles = [buf[h, 8 * g : 8 * g + 8, y, :] for g in range(GROUPS)]
            wide = jnp.concatenate(tiles[:16], axis=0).T
            upper = jnp.concatenate(tiles[16:], axis=0)
            bands = jnp.concatenate([turn(upper, -32 * q, 1) for q in range(4)], axis=0)
            bands = bands.T[:32, :]
            out[h, y, :LANES, :] = wide
            out[h, y, LANES:, :] = bands
            first[8 * h + y] = wide[:8]
            last[8 * h + y] = wide[120:]
            first[16 + 8 * h + y] = bands[:8]
            last[16 + 8 * h + y] = bands[24:]
        send(out.at[h], o_ref.at[:, pl.ds(0, NZ), :])
    loads[2].wait()
    send(fields, hi_ref.at[:, pl.ds(NZ, 8), :])
    send(first, first_ref)
    send(last, last_ref)
    wait_all(stores)


def columns_kernel(
    own_first, own_last, f_hbm, y_hbm, s_hbm, n_hbm, first_ref, last_ref,
    mine, halo, fields, edges, out, sems, out_sems,
):
    pairs = [(own_first, mine.at[0]), (own_last, mine.at[1])]
    for i, msg in enumerate((s_hbm, n_hbm)):
        for j, at in enumerate((0, 120, 128, 152)):
            pairs.append((msg.at[:, pl.ds(at, 8), :], halo.at[i, j]))
    pairs.append((s_hbm.at[:, pl.ds(NZ, 8), :], fields))
    for i, ref in enumerate((f_hbm, y_hbm)):
        pairs.append((ref.at[pl.ds(8, 2)], edges.at[i]))
    wait_all(fetch_all(pairs, sems))
    lane = lane_ids((8, LANES))
    for side in range(2):
        for y in range(8):
            out[side, y] = halo[0, side, y]
            out[side, 24 + y] = halo[1, side, y]
        for y in range(16):
            out[side, 8 + y] = mine[side, y]
        for p in range(8):
            tile = None
            for j in range(4):
                y = 4 * p + j
                if y < 8:
                    x = halo[0, 2 + side, y]
                elif y < 24:
                    x = mine[side, 16 + y - 8]
                else:
                    x = halo[1, 2 + side, y - 24]
                x = turn(x, 32 * j - 96 * side, 1)
                tile = x if j == 0 else jnp.where(lane >= 32 * j, x, tile)
            out[side, 32 + p] = tile
        out[side, 40] = edge_tile([fields[i] for i in range(8)], side == 0)
        out[side, 41] = edges[0, side]
        out[side, 42] = edges[1, side]
    wait_all(fetch_all([(out.at[0], first_ref), (out.at[1], last_ref)], out_sems))


def edges_kernel(f_ref, y_ref, o_ref):
    o_ref[0] = f_ref[8]
    o_ref[1] = y_ref[8]


def moments_kernel(f_ref, y_ref, x_ref, o_ref):
    lane8 = lane_ids((8, LANES))
    fields = []
    for f in range(4):
        main = jnp.concatenate([f_ref[2 * f], f_ref[2 * f + 1], y_ref[2 * f]], axis=0)
        extra = [
            turn(x_ref[0], -16 * (2 * f), 1),
            turn(x_ref[0], -16 * (2 * f + 1), 1),
            turn(x_ref[1], -16 * (2 * f), 1),
        ]
        extra = [jnp.where(lane8 < 16, x, 0.0) for x in extra]
        fields.append(jnp.concatenate([main, jnp.concatenate(extra, axis=0)], axis=1))
    shape = fields[0].shape
    lane, row = lane_ids(shape), row_ids(shape)
    last_x = jnp.where(lax.axis_index("gx") == 7, 127, -9)
    last_y = jnp.where(lax.axis_index("gy") == 15, 15, -9)
    keep_e = jnp.where(lane == last_x, 0.0, 1.0)
    keep_w = jnp.where(lane == last_x + 1, 0.0, 1.0)
    keep_n = jnp.where(row == last_y, 0.0, 1.0)
    keep_s = jnp.where(row == last_y + 1, 0.0, 1.0)
    apply = stencil(fields[2], fields[3], keep_e, keep_w, keep_n, keep_s)
    inside = (row >= 3) & (row < 19) & (lane >= 3) & (lane < 131)
    v0 = fields[:2]
    v1 = [apply(w) for w in v0]
    v2 = [apply(w) for w in v1]
    v3 = [apply(w) for w in v2]
    result = jnp.zeros((1, LANES), jnp.float32)
    pairs = ((v0, v0), (v0, v1), (v1, v1), (v1, v2), (v2, v2), (v2, v3))
    for j, (p, q) in enumerate(pairs):
        prod = jnp.where(inside, p[0] * q[0] + p[1] * q[1], 0.0)
        part = prod[:, :LANES] + prod[:, LANES:]
        total = jnp.sum(jnp.sum(part, axis=0, keepdims=True), axis=1, keepdims=True)
        result = jnp.where(lane_ids((1, LANES)) == j, total, result)
    rows = row_ids((LANES * COPIES, LANES))
    o_ref[...] = jnp.where(rows % COPIES == 0, jnp.broadcast_to(result, rows.shape), 0.0)


def krylov_basis(own, west, east, south, north, o_ref, t_ref):
    lane8 = lane_ids((8, LANES))
    fields = []
    for f in range(4):
        main, extra = [], []
        for t in range(6):
            i = 2 * f + t % 2
            if t < 2:
                mid = south[i]
            elif t < 4:
                mid = own[i]
            else:
                mid = north[i]
            main.append(mid)
            right = turn(east[t // 2], -16 * i, 1)
            left = turn(west[t // 2], 112 - 16 * i, 1)
            extra.append(jnp.where(lane8 < 16, right, jnp.where(lane8 >= 112, left, 0.0)))
        fields.append(
            jnp.concatenate(
                [jnp.concatenate(main, axis=0), jnp.concatenate(extra, axis=0)], axis=1
            )
        )
    shape = fields[0].shape
    lane, row = lane_ids(shape), row_ids(shape)
    low_y = jnp.where(lax.axis_index("gy") == 0, 16, 0)
    high_y = jnp.where(lax.axis_index("gy") == 15, 32, 48)
    end_x = jnp.where(lax.axis_index("gx") == 7, 128, 144)
    start_x = jnp.where(lax.axis_index("gx") == 0, 256, 240)
    inside = (row >= low_y) & (row < high_y) & ((lane < end_x) | (lane >= start_x))
    inside = jnp.where(inside, 1.0, 0.0)
    fields = [x * inside for x in fields]
    apply = stencil(fields[2], fields[3], 1.0, 1.0, 1.0, 1.0)
    vectors = [fields[:2]]
    for _ in range(2):
        vectors.append([apply(w) * inside for w in vectors[-1]])
    fill = jnp.zeros((96, LANES), jnp.float32)
    for b in range(3):
        for c in range(2):
            v = vectors[b][c]
            o_ref[c, b] = v[16:32, :LANES]
            v = turn(v[8:40, :], 8, 1)
            t_ref[c, b, :LANES] = jnp.concatenate([v[:, :LANES], fill], axis=0).T
            t_ref[c, b, LANES:] = jnp.concatenate([v[:, LANES:], fill], axis=0).T[:16, :]


def cg_coefficients(m):
    a0 = m[0] / m[1]
    rr1 = a0 * a0 * m[2] - m[0]
    b0 = rr1 / m[0]
    p1 = (1.0 + b0, -a0)
    q1 = p1[0] * p1[0] * m[1] + 2.0 * p1[0] * p1[1] * m[2] + p1[1] * p1[1] * m[3]
    a1 = rr1 / q1
    r2 = (1.0, -a0 - a1 * p1[0], -a1 * p1[1])

    def form(p, k):
        return (
            p[0] * p[0] * m[k]
            + 2.0 * p[0] * p[1] * m[k + 1]
            + (2.0 * p[0] * p[2] + p[1] * p[1]) * m[k + 2]
            + 2.0 * p[1] * p[2] * m[k + 3]
            + p[2] * p[2] * m[k + 4]
        )

    rr2 = form(r2, 0)
    b1 = rr2 / rr1
    p2 = (1.0 + b1 * p1[0], r2[1] + b1 * p1[1], r2[2])
    a2 = rr2 / form(p2, 1)
    inv = 1.0 / SCALE
    return (
        (a0 + a1 * p1[0] + a2 * p2[0]) * inv,
        (a1 * p1[1] + a2 * p2[1]) * inv,
        a2 * p2[2] * inv,
    )


def main_kernel(
    lo_ref, hi_ref, s_ref, n_ref, w_ref, x_ref, f_ref, y_ref, sums_ref, lev_ref,
    col_ref, geo_ref, drag_ref, surf_ref, melt_ref, mask_ref, basin_ref, owner_ref, e_ref,
    o_ref, vel_ref, send_ref,
    wide, band, wide_x, wide_y, band_x, band_y, flow, adv,
    west_b, east_b, basis, turned, inv, planes, masks, owner, lev,
    own_f, west_f, east_f, south_f, north_f, solved, vel, send, old,
    sems, out_sems,
):
    lane8 = lane_ids((8, LANES))
    lane1 = lane_ids((1, LANES))
    copies = []

    def fetch(src, dst):
        copy = pltpu.make_async_copy(src, dst, sems.at[len(copies)])
        copy.start()
        copies.append(copy)
        return copy

    first = [
        fetch(f_ref, own_f), fetch(w_ref.at[pl.ds(40, 3)], west_f),
        fetch(x_ref.at[pl.ds(40, 3)], east_f), fetch(s_ref.at[:, pl.ds(NZ, 8), :], south_f),
        fetch(y_ref, north_f), fetch(lev_ref, lev), fetch(col_ref, planes.at[0]),
    ]
    field_here = []
    for i, ref in enumerate((s_ref, lo_ref, hi_ref, n_ref)):
        y = pl.ds(8 * i, 8)
        field_here.append(fetch(ref.at[:, pl.ds(0, 128), :], wide.at[0, y, pl.ds(16, 128), :]))
        field_here.append(fetch(ref.at[:, pl.ds(128, 32), :], band.at[0, y, pl.ds(16, 32), :]))
    for x, ref, buf in ((8, w_ref, west_b), (144, x_ref, east_b)):
        dst = wide.at[0, :, pl.ds(x, 8), :]
        field_here.append(fetch(ref.at[pl.ds(0, 32)], dst))
        field_here.append(fetch(ref.at[pl.ds(32, 8)], buf))
    later = [
        fetch(geo_ref, planes.at[1]), fetch(drag_ref, planes.at[2]),
        fetch(surf_ref, planes.at[3]), fetch(melt_ref, planes.at[4]),
        fetch(mask_ref, masks.at[0]), fetch(basin_ref, masks.at[1]), fetch(owner_ref, owner),
        fetch(e_ref, old),
    ]
    total = jnp.sum(sums_ref[...], axis=0, keepdims=True)
    m = [
        jnp.sum(jnp.where(lane1 == j, total, 0.0), axis=1, keepdims=True) for j in range(6)
    ]
    c = cg_coefficients(m)

    def profile(k):
        height = (k.astype(jnp.float32) + 0.5) / NZ
        low = 1.0 - height
        low = low * low
        return 1.0 - low * low

    prof_w = profile(lane8)
    prof_b = profile(128 + lane8 % 32)
    wait_all(first)
    col = planes[0]
    krylov_basis(own_f, west_f, east_f, south_f, north_f, basis, turned)

    def courants(i, s):
        for j in range(53):
            k = NZ - 1 - (i * 53 + j)
            lower = col * lev[k - 1]
            one = 1.0 / (s + lower)
            inv[rows_at(k * ROWS, ROWS), :] = one
            s = 1.0 + lower * (s * one)
        for j in range(6):
            at = rows_at((i * 6 + j) * 8, 8)
            for comp, o_ref in ((0, wide_x), (1, wide_y)):
                v = c[0] * turned[comp, 0, at, :]
                v = v + c[1] * turned[comp, 1, at, :]
                v = v + c[2] * turned[comp, 2, at, :]
                v = 3.0 * v
                for y in range(1, 31):
                    one = jnp.broadcast_to(v[:, y : y + 1], (8, LANES))
                    flow[comp, y, at, :] = one
                    o_ref[y, at, :] = 0.45 * jnp.tanh(one * prof_w)
        return s

    s = lax.fori_loop(0, 3, courants, 1.0 + col * lev[NZ - 1])
    inv[0:ROWS, :] = 1.0 / s

    def band_courants(i, carry):
        for j in range(3):
            t = i * 3 + j
            for comp, o_ref in ((0, band_x), (1, band_y)):
                for y in range(1, 31):
                    one = flow[comp, y, rows_at(t * 8, 8), :]
                    for q in range(1, 4):
                        other = flow[comp, y, rows_at(t * 8 + 32 * q, 8), :]
                        one = jnp.where(lane8 >= 32 * q, other, one)
                    o_ref[y, rows_at(t * 8, 8), :] = 0.45 * jnp.tanh(one * prof_b)
        return carry

    lax.fori_loop(0, 2, band_courants, 0)

    for comp in range(2):
        v = c[0] * basis[comp, 0] + c[1] * basis[comp, 1] + c[2] * basis[comp, 2]
        vel[comp] = v
    vel_out = pltpu.make_async_copy(vel, vel_ref, out_sems.at[0])
    vel_out.start()

    for copy in field_here:
        copy.wait()
    for y in range(32):
        left = turn(band[0, y, 40:48, :], 32, 1)
        left = jnp.where(lane8 < 32, turn(west_b[y // 4], -32 * (y % 4), 1), left)
        right = turn(band[0, y, 16:24, :], 96, 1)
        right = jnp.where(lane8 >= 96, turn(east_b[y // 4], 96 - 32 * (y % 4), 1), right)
        band[0, y, 8:16, :] = left
        band[0, y, 48:56, :] = right

    def substep(buf, cx_ref, cy_ref, s, t):
        src, dst = (s - 1) % 2, s % 2
        at = pl.multiple_of(t * 8, 8)
        mid = pl.ds(at + 8, 8)

        now = buf[src, s, mid, :]
        below = now - buf[src, s - 1, mid, :]
        for y in range(s, 32 - s):
            above = buf[src, y + 1, mid, :]
            west = buf[src, y, pl.ds(at + 7, 8), :]
            east = buf[src, y, pl.ds(at + 9, 8), :]
            cx = cx_ref[y, pl.ds(at, 8), :]
            cy = cy_ref[y, pl.ds(at, 8), :]
            rise = above - now
            across = jnp.where(cx > 0.0, now - west, east - now)
            along = jnp.where(cy > 0.0, below, rise)
            buf[dst, y, mid, :] = now - cx * across - cy * along
            now, below = above, rise

    for s in range(1, STEPS):

        def tiles(i, carry, s=s):
            for j in range(6):
                substep(wide, wide_x, wide_y, s, i * 6 + j)
            for j in range(2):
                substep(band, band_x, band_y, s, i * 2 + j)
            return carry

        lax.fori_loop(0, 3, tiles, 0)

    def last_step(buf, cx_ref, cy_ref, y, t):
        src, at = (STEPS - 1) % 2, 8 * t
        now = buf[src, y, at + 8 : at + 16, :]
        west = buf[src, y, at + 7 : at + 15, :]
        east = buf[src, y, at + 9 : at + 17, :]
        below = now - buf[src, y - 1, at + 8 : at + 16, :]
        rise = buf[src, y + 1, at + 8 : at + 16, :] - now
        cx = cx_ref[y, at : at + 8, :]
        cy = cy_ref[y, at : at + 8, :]
        across = jnp.where(cx > 0.0, now - west, east - now)
        return now - cx * across - cy * jnp.where(cy > 0.0, below, rise)

    def back(i, carry):
        for j in range(4):
            y = i * 4 + j
            x = [last_step(wide, wide_x, wide_y, y + 8, t) for t in range(1, 17)]
            x = jnp.concatenate(x, axis=0).T
            for g in range(16):
                adv[pl.ds(g * 128 + y, 8, stride=16), :] = x[8 * g : 8 * g + 8, :]
        x = [
            last_step(band, band_x, band_y, i * 4 + j + 8, t)
            for j in range(4)
            for t in range(1, 5)
        ]
        x = jnp.concatenate(x, axis=0).T
        for g in range(4):
            for j in range(4):
                out = None
                for q in range(4):
                    one = x[32 * q + 8 * g : 32 * q + 8 * g + 8, :]
                    one = turn(one, 32 * (q - j), 1)
                    out = one if q == 0 else jnp.where(lane8 >= 32 * q, one, out)
                adv[pl.ds((16 + g) * 128 + i * 4 + j, 8, stride=16), :] = out
        return carry

    lax.fori_loop(0, 4, back, 0)

    wait_all(later)

    def eliminate(i, above):
        k = NZ - 1 - i
        at = rows_at(k * ROWS, ROWS)
        one = inv[at, :]
        above = adv[at, :] * one + col * lev[k] * one * above
        solved[at, :] = above
        return above

    above = lax.fori_loop(0, NZ, eliminate, planes[3], unroll=16)
    u, v = vel[0], vel[1]
    bottom = planes[1] + 10.0 * planes[2] * (u * u + v * v)
    above = above + bottom * inv[0:ROWS, :]

    melt = jnp.where(masks[0] == 1, jnp.maximum(above - planes[4], 0.0), 0.0)
    melt = jnp.sum(melt, axis=0, keepdims=True) * MEAN
    place = row_ids((LANES, LANES)) * 2 + lane_ids((LANES, LANES))
    place = jnp.where(lane_ids((LANES, LANES)) < 2, place, -1)
    slots = owner[...]
    ids = row_ids(slots.shape) * LANES + lane_ids(slots.shape)
    out = jnp.zeros((LANES, LANES), jnp.float32)
    for j in range(4):
        part = jnp.where((lane1 >= 32 * j) & (lane1 < 32 * j + 32), melt, 0.0)
        part = jnp.sum(part, axis=1, keepdims=True)
        mine = jnp.sum(jnp.where(lane1 == 32 * j, masks[1, 0:1, :], 0), axis=1, keepdims=True)
        slot = jnp.where(ids == mine, slots, 0)
        slot = jnp.sum(jnp.sum(slot, axis=0, keepdims=True), axis=1, keepdims=True)
        out = out + jnp.where(place == slot, part, 0.0)
    send[...] = out
    send_out = pltpu.make_async_copy(send, send_ref, out_sems.at[1])
    send_out.start()

    outs = [vel_out, send_out]
    ice = masks[0] == 1
    solved[0:ROWS, :] = jnp.where(ice, above, old[0:ROWS, :])

    def substitute(k, below):
        at = rows_at(k * ROWS, ROWS)
        below = solved[at, :] + col * lev[k - 1] * inv[at, :] * below
        solved[at, :] = jnp.where(ice, below, old[at, :])
        return below

    below = above
    parts = 5
    size = NZ // parts
    for part in range(parts):
        first_k = part * size
        below = lax.fori_loop(max(first_k, 1), first_k + size, substitute, below, unroll=16)
        at = pl.ds(first_k * ROWS, size * ROWS)
        copy = pltpu.make_async_copy(solved.at[at], o_ref.at[at], out_sems.at[2 + part])
        copy.start()
        outs.append(copy)
    wait_all(outs)


def hand_on(v_ref, o_ref):
    o_ref[...] = v_ref[...]


MEAN = 256 / 262144


def per_device(
    enthalpy,
    conduct_col,
    conduct_level,
    surface_enthalpy,
    geothermal,
    melt_level,
    viscosity,
    drag,
    driving_stress,
    ice_mask,
    basin,
    owner_slot,
):
    nx, ny = lax.axis_size("gx"), lax.axis_size("gy")
    both = ("gx", "gy")
    up_x = [(i, i + 1) for i in range(nx - 1)]
    down_x = [(i + 1, i) for i in range(nx - 1)]
    ring_x = [((i + 1) % nx, i) for i in range(nx)]
    up_y = [(i, i + 1) for i in range(ny - 1)]
    down_y = [(i + 1, i) for i in range(ny - 1)]
    ring_y = [((i + 1) % ny, i) for i in range(ny)]
    dma = pltpu.SemaphoreType.DMA

    def vmem(*shape, dtype=jnp.float32):
        return pltpu.VMEM(shape, dtype)

    tie = lax.optimization_barrier

    with jax.named_scope("fields"):
        (fields,) = call(
            fields_kernel, [f32(10, 8, LANES)], driving_stress, viscosity, drag,
            places="aaa" + "a",
            scratch=(vmem(4, ROWS, LANES), vmem(10, 8, LANES), dma((3,))),
            limit=MOST,
        )
        rows = lax.ppermute(fields, "gy", ring_y)
    with jax.named_scope("levels_on_lanes"):
        low, high, first, last = call(
            transpose_kernel,
            [f32(8, LOW, LANES), f32(8, HIGH, LANES)] + [f32(32, 8, LANES)] * 2,
            enthalpy, fields, places="aa" + "aaaa",
            scratch=(
                vmem(2, NZ, 8, LANES), vmem(2, 8, NZ, LANES), vmem(8, 8, LANES),
                vmem(32, 8, LANES), vmem(32, 8, LANES), dma((3,)), dma((5,)),
            ),
            limit=FULL,
        )
    with jax.named_scope("moments"):
        (message,) = call(
            edges_kernel, [f32(2, 8, LANES)], fields, rows, places="vv" + "v", limit=SMALL
        )
        edge = lax.ppermute(message, "gx", ring_x)
        (sums,) = call(
            moments_kernel, [f32(LANES * COPIES, LANES)], fields, rows, edge, places="vvv" + "v",
            limit=SMALL,
        )

    with jax.named_scope("halo"):
        high_out, low_out, _ = tie((high, low, message))
        south = lax.ppermute(high_out, "gy", up_y)
        north = lax.ppermute(low_out, "gy", down_y)

    with jax.named_scope("moments"):
        every = lax.all_to_all(sums.reshape(LANES, COPIES, LANES), both, 0, 0)
        every = every.reshape(LANES * COPIES, LANES)

    with jax.named_scope("halo"):
        first, last, _ = tie((first, last, sums))
        first, last = call(
            columns_kernel, [f32(43, 8, LANES)] * 2,
            first, last, fields, rows, south, north, places="aaaaaa" + "aa",
            scratch=(
                vmem(2, 32, 8, LANES), vmem(2, 4, 8, 8, LANES), vmem(8, 8, LANES),
                vmem(2, 2, 8, LANES), vmem(2, 43, 8, LANES), dma((13,)), dma((2,)),
            ),
            limit=FULL, cost=0,
        )
        east = lax.ppermute(first, "gx", down_x)
        west = lax.ppermute(last, "gx", up_x)

    with jax.named_scope("transport"):
        solved, velocity, send = call(
            main_kernel,
            [f32(NZ * ROWS, LANES), f32(2, ROWS, LANES), f32(LANES, LANES)],
            low, high, south, north, west, east, fields, rows, every, conduct_level,
            conduct_col, geothermal, drag, surface_enthalpy, melt_level, ice_mask, basin,
            owner_slot.reshape(2, LANES), enthalpy.reshape(NZ * ROWS, LANES),
            places="aaaavvaa" + "v" + "a" * 10 + "aaa",
            scratch=(
                vmem(2, 32, WIDE + 16, LANES), vmem(2, 32, BAND + 16, LANES),
                vmem(32, WIDE, LANES), vmem(32, WIDE, LANES),
                vmem(32, BAND, LANES), vmem(32, BAND, LANES),
                vmem(2, 32, WIDE, LANES), vmem(NZ * ROWS, LANES),
                vmem(8, 8, LANES), vmem(8, 8, LANES),
                vmem(2, 3, ROWS, LANES), vmem(2, 3, WIDE, LANES),
                vmem(NZ * ROWS, LANES), vmem(5, ROWS, LANES),
                vmem(2, ROWS, LANES, dtype=jnp.int32), vmem(2, LANES, dtype=jnp.int32),
                pltpu.SMEM((NZ,), jnp.float32),
                vmem(10, 8, LANES), vmem(3, 8, LANES), vmem(3, 8, LANES), vmem(8, 8, LANES),
                vmem(10, 8, LANES),
                vmem(NZ * ROWS, LANES), vmem(2, ROWS, LANES), vmem(LANES, LANES),
                vmem(NZ * ROWS, LANES),
                dma((32,)), dma((8,)),
            ),
            limit=MOST,
        )

    with jax.named_scope("basin_melt"):
        received = lax.all_to_all(send.reshape(LANES, 1, LANES), both, 0, 0)
        basin_melt = jnp.sum(received.reshape(LANES, LANES)[:, :2], axis=0)
        (velocity,) = call(
            hand_on, [f32(2, ROWS, LANES)], velocity, places="vd", limit=SMALL, cost=1 << 23
        )

    return (solved.reshape(NZ, ROWS, LANES), velocity, basin_melt)


def solution(mesh):
    return jax.shard_map(
        per_device,
        mesh=mesh,
        in_specs=(
            P(None, "gy", "gx"),
            P("gy", "gx"),
            P(),
            P("gy", "gx"),
            P("gy", "gx"),
            P("gy", "gx"),
            P("gy", "gx"),
            P("gy", "gx"),
            P(None, "gy", "gx"),
            P("gy", "gx"),
            P("gy", "gx"),
            P(),
        ),
        out_specs=(P(None, "gy", "gx"), P(None, "gy", "gx"), P(("gx", "gy"))),
        check_vma=False,
    )
```

time: 84.9 us -> 81.1 us (0.955)
  Pallas kernels: 31.6 us -> 23.3 us
  starting transfers between devices: 32.8 us -> 38.2 us
  local copies, waits for them, and re-layouts: 4.42 us -> 1.4 us
  waiting for transfers between devices: 14.1 us -> 16.4 us
    pallas_call x9 -> x7, Pallas kernels: 31.6 us -> 23.3 us  [call(): pl.pallas_call(kernel, out_shape=outs, in_specs=specs[:len(args)], out_sp...]
    ppermute x3 -> x4, starting transfers between devices: 2.65 us -> 6.34 us  [the longest x1 2.17 us: per_device(): south = lax.ppermute(high_out, 'gy', up_y)]
    unnamed x24 -> x12, local copies, waits for them, and re-layouts: 4.42 us -> 1.4 us
    ppermute x3 -> x4, waiting for transfers between devices: 2.86 us -> 5.73 us  [the longest x1 2.87 us: per_device(): east = lax.ppermute(first, 'gx', down_x)]
    ppermute x1, waiting for transfers between devices: 2.29 us -> 0.01 us  [per_device(): west = lax.ppermute(last, 'gx', up_x)]
    all_to_all x1, waiting for transfers between devices: 6.31 us -> 8.44 us  [per_device(): received = lax.all_to_all(send.reshape(LANES, 1, LANES), both, 0, 0)]
    ppermute x1, starting transfers between devices: 3.96 us -> 4.87 us  [per_device(): west = lax.ppermute(last, 'gx', up_x)]
    all_to_all x1, starting transfers between devices: 10.3 us -> 11.2 us  [per_device(): every = lax.all_to_all(sums.reshape(LANES, COPIES, LANES), both, 0, 0)]
  transfers between devices with their start and end apart: 7 -> 8, of which waited for: 5 -> 5; matrix products, arithmetic and copies ran while one was open for 0% -> 0% of each run, Pallas kernels for 16% -> 9%
where the time goes in v1:
time: 81.1 us; the launch traced here: 80.6 us
  starting transfers between devices  38.2 us (47%)
  Pallas kernels  23.3 us (29%)
  waiting for transfers between devices  16.4 us (20%)
  local copies, waits for them, and re-layouts  1.4 us (2%)
    pallas_call x7, Pallas kernels, call(): pl.pallas_call(kernel, out_shape=outs, in_specs=specs[:len(args)], out_sp...  23.3 us
    all_to_all x1, starting transfers between devices, per_device(): every = lax.all_to_all(sums.reshape(LANES, COPIES, LANES), both, 0, 0)  11.2 us
    all_to_all x1, starting transfers between devices, per_device(): received = lax.all_to_all(send.reshape(LANES, 1, LANES), both, 0, 0)  8.71 us
    all_to_all x1, waiting for transfers between devices, per_device(): received = lax.all_to_all(send.reshape(LANES, 1, LANES), both, 0, 0)  8.44 us
    ppermute x1, starting transfers between devices, per_device(): rows = lax.ppermute(fields, 'gy', ring_y)  7.11 us
    ppermute x1, starting transfers between devices, per_device(): west = lax.ppermute(last, 'gx', up_x)  4.87 us
    ppermute x1, waiting for transfers between devices, per_device(): east = lax.ppermute(first, 'gx', down_x)  2.87 us
    ppermute x1, waiting for transfers between devices, per_device(): edge = lax.ppermute(message, 'gx', ring_x)  2.43 us
  transfers between devices with their start and end apart: 8, of which 5 were waited for; matrix products, arithmetic and copies ran while one was open for 0% of the time, Pallas kernels for 9%

profile of v1, /device:TPU:1, one launch (start us, length us, event | category | flops | bytes accessed | tf_op | source)
XLA Modules:
  0.0 80.6 jit_solution(15995110839594006520)
XLA Ops:
  0.6 1.4 %fields.1.f_ref.f_hbm = f32[10,8,128]{2,1,0:T(8,128)} custom-call(f32[2,16,128]{2,1,0:T(8,128)} %stress_ref.1, f32[16,128]{1,0:T(8,128)} %visc_ref.1, f32[16,128]{1,0:T(8,128)} %drag_ref.3), custom_call_target="tpu_custom_call" | custom-call | bytes 73728 | tf_op jit(solution)/shard_map/fields/pallas_call | solution.py:47
  2.1 0.0 copy-start
  2.1 7.1 %collective-permute-start = (f32[10,8,128]{2,1,0:T(8,128)}, f32[10,8,128]{2,1,0:T(8,128)S(1)}, u32[]{:S(2)}, u32[]{:S(2)}) collective-permute-start(f32[10,8,128]{2,1,0:T(8,128)} %fields.1.f_ref.f_hbm), channel_id=1, source_target_pairs={{1,0},{2,1},{3,2},{4,3},{5,4},{6,5},{7,6},{8,7},{9,8},{10,9},{11,1... | collective-permute-start | bytes 122888 | tf_op jit(solution)/shard_map/fields/ppermute | solution.py:601
  9.2 3.1 %levels_on_lanes.1 = (f32[8,160,128]{2,1,0:T(8,128)}, f32[8,168,128]{2,1,0:T(8,128)}, f32[32,8,128]{2,1,0:T(8,128)}, f32[32,8,128]{2,1,0:T(8,128)}) custom-call(f32[160,16,128]{2,1,0:T(8,128)} %e_ref.1, f32[10,8,128]{2,1,0:T(8,128)} %fields.1.f_ref.f_hbm), custom_call_target="tpu_custom_call" | custom-call | bytes 2957312 | tf_op jit(solution)/shard_map/levels_on_lanes/pallas_call | solution.py:47
  12.3 0.0 collective-permute-done.y_ref.y_hbm
  12.3 0.0 copy-done
  12.3 0.0 copy-start.1
  12.3 2.2 %collective-permute-start.1 = (f32[8,168,128]{2,1,0:T(8,128)}, f32[8,168,128]{2,1,0:T(8,128)}, u32[]{:S(2)}, u32[]{:S(2)}) collective-permute-start(f32[8,168,128]{2,1,0:T(8,128)} %get-tuple-element.18.hi_ref), channel_id=1, source_target_pairs={{0,1},{1,2},{2,3},{3,4},{4,5},{5,6},{6,7},{7,8},{8,9},{9,10},{10,1... | collective-permute-start | bytes 2064392 | tf_op jit(solution)/shard_map/halo/ppermute | solution.py:625
  14.5 1.3 %collective-permute-start.2 = (f32[8,160,128]{2,1,0:T(8,128)}, f32[8,160,128]{2,1,0:T(8,128)}, u32[]{:S(2)}, u32[]{:S(2)}) collective-permute-start(f32[8,160,128]{2,1,0:T(8,128)} %get-tuple-element.19.lo_ref), channel_id=1, source_target_pairs={{1,0},{2,1},{3,2},{4,3},{5,4},{6,5},{7,6},{8,7},{9,8},{10,9},{11,1... | collective-permute-start | bytes 1966088 | tf_op jit(solution)/shard_map/halo/ppermute | solution.py:626
  15.8 1.0 %collective-permute-start.3 = (f32[2,8,128]{2,1,0:T(8,128)S(1)}, f32[2,8,128]{2,1,0:T(8,128)S(1)}, u32[]{:S(2)}, u32[]{:S(2)}) collective-permute-start(f32[2,8,128]{2,1,0:T(8,128)S(1)} %moments.2), channel_id=1, source_target_pairs={{16,0},{32,16},{48,32},{64,48},{80,64},{96,80},{112,96},{0,112},{1... | collective-permute-start | bytes 24584 | tf_op jit(solution)/shard_map/moments/ppermute | solution.py:617
  16.7 2.4 %collective-permute-done.3.x_ref = f32[2,8,128]{2,1,0:T(8,128)S(1)} collective-permute-done((f32[2,8,128]{2,1,0:T(8,128)S(1)}, f32[2,8,128]{2,1,0:T(8,128)S(1)}, u32[]{:S(2)}, u32[]{:S(2)}) %collective-permute-start.3) | collective-permute-done | bytes 8224 | tf_op jit(solution)/shard_map/moments/ppermute | solution.py:617
  19.2 1.2 %moments.3 = f32[512,128]{1,0:T(8,128)} custom-call(f32[10,8,128]{2,1,0:T(8,128)S(1)} %copy-done, f32[10,8,128]{2,1,0:T(8,128)S(1)} %collective-permute-done.y_ref.y_hbm, f32[2,8,128]{2,1,0:T(8,128)S(1)} %collective-permute-done.3.x_ref), custom_call_target="tpu_custom_call" | custom-call | bytes 352256 | tf_op jit(solution)/shard_map/moments/pallas_call | solution.py:47
  20.3 11.2 %all-to-all-start = ((f32[128,4,128]{2,1,0:T(4,128)}), f32[128,4,128]{2,1,0:T(4,128)S(1)}, u32[]{:S(2)}, u32[]{:S(2)}) async-start(f32[128,4,128]{2,1,0:T(4,128)} %bitcast), calls=%async_computation | async-start | bytes 524288 | tf_op jit(solution)/shard_map/moments/all_to_all | solution.py:629
  31.5 0.4 collective-permute-done.2.n_hbm.n_ref
  32.0 0.0 collective-permute-done.1.s_hbm.s_ref
  32.0 0.0 copy-done.1
  32.0 2.0 %halo.1 = (f32[43,8,128]{2,1,0:T(8,128)}, f32[43,8,128]{2,1,0:T(8,128)}) custom-call(f32[32,8,128]{2,1,0:T(8,128)} %get-tuple-element.22.own_first, f32[32,8,128]{2,1,0:T(8,128)} %get-tuple-element.23.own_last, f32[10,8,128]{2,1,0:T(8,128)} %fields.1.f_ref.f_hbm, f32[10,8,128]{2,1,0:T(8,128)} %copy-done.1, ...), custom_call_target="tpu_custom_call" | custom-call | tf_op jit(solution)/shard_map/halo/pallas_call | solution.py:47
  34.0 4.9 %collective-permute-start.4 = (f32[43,8,128]{2,1,0:T(8,128)}, f32[43,8,128]{2,1,0:T(8,128)S(1)}, u32[]{:S(2)}, u32[]{:S(2)}) collective-permute-start(f32[43,8,128]{2,1,0:T(8,128)} %get-tuple-element.24), channel_id=1, source_target_pairs={{0,16},{16,32},{32,48},{48,64},{64,80},{80,96},{96,112},{1,17},{17... | collective-permute-start | bytes 528392 | tf_op jit(solution)/shard_map/halo/ppermute | solution.py:644
  38.9 1.9 %collective-permute-start.5 = (f32[43,8,128]{2,1,0:T(8,128)}, f32[43,8,128]{2,1,0:T(8,128)S(1)}, u32[]{:S(2)}, u32[]{:S(2)}) collective-permute-start(f32[43,8,128]{2,1,0:T(8,128)} %get-tuple-element.25), channel_id=1, source_target_pairs={{16,0},{32,16},{48,32},{64,48},{80,64},{96,80},{112,96},{17,1},{33... | collective-permute-start | bytes 528392 | tf_op jit(solution)/shard_map/halo/ppermute | solution.py:643
  40.8 2.2 %all-to-all-done = f32[128,4,128]{2,1,0:T(4,128)S(1)} async-done(((f32[128,4,128]{2,1,0:T(4,128)}), f32[128,4,128]{2,1,0:T(4,128)S(1)}, u32[]{:S(2)}, u32[]{:S(2)}) %all-to-all-start) | async-done | bytes 262176 | tf_op jit(solution)/shard_map/moments/all_to_all | solution.py:629
  43.0 0.0 copy-start.3
  43.0 0.0 collective-permute-done.4.w_ref
  43.0 0.0 copy-start.4
  43.0 2.9 %collective-permute-done.5.x_ref = f32[43,8,128]{2,1,0:T(8,128)S(1)} collective-permute-done((f32[43,8,128]{2,1,0:T(8,128)}, f32[43,8,128]{2,1,0:T(8,128)S(1)}, u32[]{:S(2)}, u32[]{:S(2)}) %collective-permute-start.5) | collective-permute-done | bytes 176160 | tf_op jit(solution)/shard_map/halo/ppermute | solution.py:643
  45.9 0.0 copy-start.5
  45.9 0.0 copy-done.3
  45.9 0.0 copy-done.4
  45.9 0.7 copy-done.5
  46.5 15.0 %transport.1 = (f32[2560,128]{1,0:T(8,128)}, f32[2,16,128]{2,1,0:T(8,128)}, f32[128,128]{1,0:T(8,128)}) custom-call(f32[8,160,128]{2,1,0:T(8,128)} %get-tuple-element.19.lo_ref, f32[8,168,128]{2,1,0:T(8,128)} %get-tuple-element.18.hi_ref, f32[8,168,128]{2,1,0:T(8,128)} %collective-permute-done.1.s_hbm.s_ref, ...), custom_call_target="tpu_custom_call" | custom-call | bytes 6145664 | tf_op jit(solution)/shard_map/transport/pallas_call | solution.py:47
  61.5 8.7 %all-to-all-start.1 = ((f32[128,1,128]{2,1,0:T(1,128)}), f32[128,1,128]{2,1,0:T(1,128)S(1)}, u32[]{:S(2)}, u32[]{:S(2)}) async-start(f32[128,1,128]{2,1,0:T(1,128)} %bitcast.12), calls=%async_computation.1 | async-start | bytes 131072 | tf_op jit(solution)/shard_map/basin_melt/all_to_all | solution.py:674
  70.3 0.0 copy-start.2
  70.3 0.7 copy-done.2
  71.0 0.6 basin_melt.1
  71.6 8.4 %all-to-all-done.1 = f32[128,1,128]{2,1,0:T(1,128)S(1)} async-done(((f32[128,1,128]{2,1,0:T(1,128)}), f32[128,1,128]{2,1,0:T(1,128)S(1)}, u32[]{:S(2)}, u32[]{:S(2)}) %all-to-all-start.1) | async-done | bytes 65568 | tf_op jit(solution)/shard_map/basin_melt/all_to_all | solution.py:674
  80.0 0.5 slice_reduce_fusion
  (1 shorter events, 0.0 us)
Async XLA Ops:
  2.1 10.2 %copy-start = (f32[10,8,128]{2,1,0:T(8,128)S(1)}, f32[10,8,128]{2,1,0:T(8,128)}, u32[]{:S(2)}) copy-start(f32[10,8,128]{2,1,0:T(8,128)} %fields.1.f_ref.f_hbm) | copy-start | bytes 122884
  2.1 10.2 %collective-permute-start = (f32[10,8,128]{2,1,0:T(8,128)}, f32[10,8,128]{2,1,0:T(8,128)S(1)}, u32[]{:S(2)}, u32[]{:S(2)}) collective-permute-start(f32[10,8,128]{2,1,0:T(8,128)} %fields.1.f_ref.f_hbm), channel_id=1, source_target_pairs={{1,0},{2,1},{3,2},{4,3},{5,4},{6,5},{7,6},{8,7},{9,8},{10,9},{11,1... | collective-permute-start | bytes 122888 | tf_op jit(solution)/shard_map/fields/ppermute | solution.py:601
  12.3 19.7 %copy-start.1 = (f32[10,8,128]{2,1,0:T(8,128)}, f32[10,8,128]{2,1,0:T(8,128)S(1)}, u32[]{:S(2)}) copy-start(f32[10,8,128]{2,1,0:T(8,128)S(1)} %collective-permute-done.y_ref.y_hbm) | copy-start | bytes 122884
  12.3 19.7 %collective-permute-start.1 = (f32[8,168,128]{2,1,0:T(8,128)}, f32[8,168,128]{2,1,0:T(8,128)}, u32[]{:S(2)}, u32[]{:S(2)}) collective-permute-start(f32[8,168,128]{2,1,0:T(8,128)} %get-tuple-element.18.hi_ref), channel_id=1, source_target_pairs={{0,1},{1,2},{2,3},{3,4},{4,5},{5,6},{6,7},{7,8},{8,9},{9,10},{10,1... | collective-permute-start | bytes 2064392 | tf_op jit(solution)/shard_map/halo/ppermute | solution.py:625
  14.5 17.5 %collective-permute-start.2 = (f32[8,160,128]{2,1,0:T(8,128)}, f32[8,160,128]{2,1,0:T(8,128)}, u32[]{:S(2)}, u32[]{:S(2)}) collective-permute-start(f32[8,160,128]{2,1,0:T(8,128)} %get-tuple-element.19.lo_ref), channel_id=1, source_target_pairs={{1,0},{2,1},{3,2},{4,3},{5,4},{6,5},{7,6},{8,7},{9,8},{10,9},{11,1... | collective-permute-start | bytes 1966088 | tf_op jit(solution)/shard_map/halo/ppermute | solution.py:626
  15.8 3.4 %collective-permute-start.3 = (f32[2,8,128]{2,1,0:T(8,128)S(1)}, f32[2,8,128]{2,1,0:T(8,128)S(1)}, u32[]{:S(2)}, u32[]{:S(2)}) collective-permute-start(f32[2,8,128]{2,1,0:T(8,128)S(1)} %moments.2), channel_id=1, source_target_pairs={{16,0},{32,16},{48,32},{64,48},{80,64},{96,80},{112,96},{0,112},{1... | collective-permute-start | bytes 24584 | tf_op jit(solution)/shard_map/moments/ppermute | solution.py:617
  20.3 22.6 %all-to-all-start = ((f32[128,4,128]{2,1,0:T(4,128)}), f32[128,4,128]{2,1,0:T(4,128)S(1)}, u32[]{:S(2)}, u32[]{:S(2)}) async-start(f32[128,4,128]{2,1,0:T(4,128)} %bitcast), calls=%async_computation | async-start | bytes 524288 | tf_op jit(solution)/shard_map/moments/all_to_all | solution.py:629
  34.0 9.0 %collective-permute-start.4 = (f32[43,8,128]{2,1,0:T(8,128)}, f32[43,8,128]{2,1,0:T(8,128)S(1)}, u32[]{:S(2)}, u32[]{:S(2)}) collective-permute-start(f32[43,8,128]{2,1,0:T(8,128)} %get-tuple-element.24), channel_id=1, source_target_pairs={{0,16},{16,32},{32,48},{48,64},{64,80},{80,96},{96,112},{1,17},{17... | collective-permute-start | bytes 528392 | tf_op jit(solution)/shard_map/halo/ppermute | solution.py:644
  38.9 7.0 %collective-permute-start.5 = (f32[43,8,128]{2,1,0:T(8,128)}, f32[43,8,128]{2,1,0:T(8,128)S(1)}, u32[]{:S(2)}, u32[]{:S(2)}) collective-permute-start(f32[43,8,128]{2,1,0:T(8,128)} %get-tuple-element.25), channel_id=1, source_target_pairs={{16,0},{32,16},{48,32},{64,48},{80,64},{96,80},{112,96},{17,1},{33... | collective-permute-start | bytes 528392 | tf_op jit(solution)/shard_map/halo/ppermute | solution.py:643
  43.0 2.9 %copy-start.3 = (f32[128,4,128]{2,1,0:T(4,128)}, f32[128,4,128]{2,1,0:T(4,128)S(1)}, u32[]{:S(2)}) copy-start(f32[128,4,128]{2,1,0:T(4,128)S(1)} %all-to-all-done) | copy-start | bytes 786436
  43.0 2.9 %copy-start.4 = (f32[43,8,128]{2,1,0:T(8,128)}, f32[43,8,128]{2,1,0:T(8,128)S(1)}, u32[]{:S(2)}) copy-start(f32[43,8,128]{2,1,0:T(8,128)S(1)} %collective-permute-done.4.w_ref) | copy-start | bytes 528388
  45.9 0.7 copy-start.5
  61.5 18.5 %all-to-all-start.1 = ((f32[128,1,128]{2,1,0:T(1,128)}), f32[128,1,128]{2,1,0:T(1,128)S(1)}, u32[]{:S(2)}, u32[]{:S(2)}) async-start(f32[128,1,128]{2,1,0:T(1,128)} %bitcast.12), calls=%async_computation.1 | async-start | bytes 131072 | tf_op jit(solution)/shard_map/basin_melt/all_to_all | solution.py:674
  70.3 0.7 copy-start.2

commit v2 on v1

--- a/solution.py
+++ b/solution.py
@@ -100,13 +100,26 @@
     return out
 
 
+def start_copy(src, dst, sem):
+    if not isinstance(src, tuple) and not isinstance(dst, tuple):
+        copy = pltpu.make_async_copy(src, dst, sem)
+        copy.start()
+        return copy
+    src = src if isinstance(src, tuple) else (src, src)
+    dst = dst if isinstance(dst, tuple) else (dst, dst)
+    odd = lax.rem(lax.axis_index("gy"), 2)
+    copies = [pltpu.make_async_copy(src[p], dst[p], sem) for p in range(2)]
+    for p in range(2):
+
+        @pl.when(odd == p)
+        def _(p=p):
+            copies[p].start()
+
+    return copies[0]
+
+
 def fetch_all(pairs, sems):
-    copies = [
-        pltpu.make_async_copy(src, dst, sems.at[i]) for i, (src, dst) in enumerate(pairs)
-    ]
-    for copy in copies:
-        copy.start()
-    return copies
+    return [start_copy(src, dst, sems.at[i]) for i, (src, dst) in enumerate(pairs)]
 
 
 def wait_all(copies):
@@ -125,12 +138,11 @@
     wait_all(fetch_all([(out, f_ref)], sems))
 
 
-LOW = 160
-HIGH = 168
+ALONG = 168
 
 
 def transpose_kernel(
-    e_ref, f_ref, lo_ref, hi_ref, first_ref, last_ref,
+    e_ref, f_ref, one_ref, two_ref, first_ref, last_ref,
     buf, out, fields, first, last, in_sems, out_sems,
 ):
     loads = fetch_all(
@@ -141,11 +153,10 @@
     stores = []
 
     def send(src, dst):
-        copy = pltpu.make_async_copy(src, dst, out_sems.at[len(stores)])
-        copy.start()
-        stores.append(copy)
-
-    for h, o_ref in ((0, lo_ref), (1, hi_ref)):
+        stores.append(start_copy(src, dst, out_sems.at[len(stores)]))
+
+    rows = [ref.at[:, pl.ds(0, NZ), :] for ref in (one_ref, two_ref)]
+    for h in range(2):
         loads[h].wait()
         for y in range(8):
             tiles = [buf[h, 8 * g : 8 * g + 8, y, :] for g in range(GROUPS)]
@@ -159,23 +170,29 @@
             last[8 * h + y] = wide[120:]
             first[16 + 8 * h + y] = bands[:8]
             last[16 + 8 * h + y] = bands[24:]
-        send(out.at[h], o_ref.at[:, pl.ds(0, NZ), :])
+        send(out.at[h], (rows[1 - h], rows[h]))
     loads[2].wait()
-    send(fields, hi_ref.at[:, pl.ds(NZ, 8), :])
+    send(fields, one_ref.at[:, pl.ds(NZ, 8), :])
+    send(fields, two_ref.at[:, pl.ds(NZ, 8), :])
     send(first, first_ref)
     send(last, last_ref)
     wait_all(stores)
 
 
 def columns_kernel(
-    own_first, own_last, f_hbm, y_hbm, s_hbm, n_hbm, first_ref, last_ref,
+    own_first, own_last, f_hbm, y_hbm, one_hbm, two_hbm, first_ref, last_ref,
     mine, halo, fields, edges, out, sems, out_sems,
 ):
     pairs = [(own_first, mine.at[0]), (own_last, mine.at[1])]
-    for i, msg in enumerate((s_hbm, n_hbm)):
+    south, north = (two_hbm, one_hbm), (one_hbm, two_hbm)
+
+    def rows_of(pair, at):
+        return tuple(msg.at[:, pl.ds(at, 8), :] for msg in pair)
+
+    for i, pair in enumerate((south, north)):
         for j, at in enumerate((0, 120, 128, 152)):
-            pairs.append((msg.at[:, pl.ds(at, 8), :], halo.at[i, j]))
-    pairs.append((s_hbm.at[:, pl.ds(NZ, 8), :], fields))
+            pairs.append((rows_of(pair, at), halo.at[i, j]))
+    pairs.append((rows_of(south, NZ), fields))
     for i, ref in enumerate((f_hbm, y_hbm)):
         pairs.append((ref.at[pl.ds(8, 2)], edges.at[i]))
     wait_all(fetch_all(pairs, sems))
@@ -323,7 +340,7 @@
 
 
 def main_kernel(
-    lo_ref, hi_ref, s_ref, n_ref, w_ref, x_ref, f_ref, y_ref, sums_ref, lev_ref,
+    own_one, own_two, one_ref, two_ref, w_ref, x_ref, f_ref, y_ref, sums_ref, lev_ref,
     col_ref, geo_ref, drag_ref, surf_ref, melt_ref, mask_ref, basin_ref, owner_ref, e_ref,
     o_ref, vel_ref, send_ref,
     wide, band, wide_x, wide_y, band_x, band_y, flow, adv,
@@ -336,21 +353,25 @@
     copies = []
 
     def fetch(src, dst):
-        copy = pltpu.make_async_copy(src, dst, sems.at[len(copies)])
-        copy.start()
-        copies.append(copy)
-        return copy
+        copies.append(start_copy(src, dst, sems.at[len(copies)]))
+        return copies[-1]
+
+    def rows_of(pair, at, size):
+        return tuple(msg.at[:, pl.ds(at, size), :] for msg in pair)
+
+    south, north = (two_ref, one_ref), (one_ref, two_ref)
+    low, high = (own_two, own_one), (own_one, own_two)
 
     first = [
         fetch(f_ref, own_f), fetch(w_ref.at[pl.ds(40, 3)], west_f),
-        fetch(x_ref.at[pl.ds(40, 3)], east_f), fetch(s_ref.at[:, pl.ds(NZ, 8), :], south_f),
+        fetch(x_ref.at[pl.ds(40, 3)], east_f), fetch(rows_of(south, NZ, 8), south_f),
         fetch(y_ref, north_f), fetch(lev_ref, lev), fetch(col_ref, planes.at[0]),
     ]
     field_here = []
-    for i, ref in enumerate((s_ref, lo_ref, hi_ref, n_ref)):
+    for i, pair in enumerate((south, low, high, north)):
         y = pl.ds(8 * i, 8)
-        field_here.append(fetch(ref.at[:, pl.ds(0, 128), :], wide.at[0, y, pl.ds(16, 128), :]))
-        field_here.append(fetch(ref.at[:, pl.ds(128, 32), :], band.at[0, y, pl.ds(16, 32), :]))
+        field_here.append(fetch(rows_of(pair, 0, LANES), wide.at[0, y, pl.ds(16, LANES), :]))
+        field_here.append(fetch(rows_of(pair, LANES, 32), band.at[0, y, pl.ds(16, 32), :]))
     for x, ref, buf in ((8, w_ref, west_b), (144, x_ref, east_b)):
         dst = wide.at[0, :, pl.ds(x, 8), :]
         field_here.append(fetch(ref.at[pl.ds(0, 32)], dst))
@@ -424,6 +445,13 @@
 
     for copy in field_here:
         copy.wait()
+    for axis, end, x, buf in (("gx", 0, 8, west_b), ("gx", 7, 144, east_b)):
+
+        @pl.when(lax.axis_index(axis) == end)
+        def _(x=x, buf=buf):
+            wide[0, :, x : x + 8, :] = jnp.zeros((32, 8, LANES), jnp.float32)
+            buf[...] = jnp.zeros((8, 8, LANES), jnp.float32)
+
     for y in range(32):
         left = turn(band[0, y, 40:48, :], 32, 1)
         left = jnp.where(lane8 < 32, turn(west_b[y // 4], -32 * (y % 4), 1), left)
@@ -431,6 +459,14 @@
         right = jnp.where(lane8 >= 96, turn(east_b[y // 4], 96 - 32 * (y % 4), 1), right)
         band[0, y, 8:16, :] = left
         band[0, y, 48:56, :] = right
+
+    for end, y in ((0, 0), (15, 24)):
+
+        @pl.when(lax.axis_index("gy") == end)
+        def _(y=y):
+            for j in range(8):
+                wide[0, y + j, 8:152, :] = jnp.zeros((WIDE, LANES), jnp.float32)
+                band[0, y + j, 8:56, :] = jnp.zeros((BAND, LANES), jnp.float32)
 
     def substep(buf, cx_ref, cy_ref, s, t):
         src, dst = (s - 1) % 2, s % 2
@@ -578,11 +614,8 @@
 ):
     nx, ny = lax.axis_size("gx"), lax.axis_size("gy")
     both = ("gx", "gy")
-    up_x = [(i, i + 1) for i in range(nx - 1)]
-    down_x = [(i + 1, i) for i in range(nx - 1)]
+    up_x = [(i, (i + 1) % nx) for i in range(nx)]
     ring_x = [((i + 1) % nx, i) for i in range(nx)]
-    up_y = [(i, i + 1) for i in range(ny - 1)]
-    down_y = [(i + 1, i) for i in range(ny - 1)]
     ring_y = [((i + 1) % ny, i) for i in range(ny)]
     dma = pltpu.SemaphoreType.DMA
 
@@ -600,13 +633,13 @@
         )
         rows = lax.ppermute(fields, "gy", ring_y)
     with jax.named_scope("levels_on_lanes"):
-        low, high, first, last = call(
+        own_one, own_two, first, last = call(
             transpose_kernel,
-            [f32(8, LOW, LANES), f32(8, HIGH, LANES)] + [f32(32, 8, LANES)] * 2,
+            [f32(8, ALONG, LANES)] * 2 + [f32(32, 8, LANES)] * 2,
             enthalpy, fields, places="aa" + "aaaa",
             scratch=(
                 vmem(2, NZ, 8, LANES), vmem(2, 8, NZ, LANES), vmem(8, 8, LANES),
-                vmem(32, 8, LANES), vmem(32, 8, LANES), dma((3,)), dma((5,)),
+                vmem(32, 8, LANES), vmem(32, 8, LANES), dma((3,)), dma((6,)),
             ),
             limit=FULL,
         )
@@ -621,9 +654,12 @@
         )
 
     with jax.named_scope("halo"):
-        high_out, low_out, _ = tie((high, low, message))
-        south = lax.ppermute(high_out, "gy", up_y)
-        north = lax.ppermute(low_out, "gy", down_y)
+        one, two, _ = tie((own_one, own_two, message))
+        one = lax.ppermute(one, "gy", [(i, i ^ 1) for i in range(ny)])
+        ends = (0, ny - 1)
+        two = lax.ppermute(
+            two, "gy", [(i, i if i in ends else ((i + 1) ^ 1) - 1) for i in range(ny)]
+        )
 
     with jax.named_scope("moments"):
         every = lax.all_to_all(sums.reshape(LANES, COPIES, LANES), both, 0, 0)
@@ -633,21 +669,21 @@
         first, last, _ = tie((first, last, sums))
         first, last = call(
             columns_kernel, [f32(43, 8, LANES)] * 2,
-            first, last, fields, rows, south, north, places="aaaaaa" + "aa",
+            first, last, fields, rows, one, two, places="aaaaaa" + "aa",
             scratch=(
                 vmem(2, 32, 8, LANES), vmem(2, 4, 8, 8, LANES), vmem(8, 8, LANES),
                 vmem(2, 2, 8, LANES), vmem(2, 43, 8, LANES), dma((13,)), dma((2,)),
             ),
             limit=FULL, cost=0,
         )
-        east = lax.ppermute(first, "gx", down_x)
+        east = lax.ppermute(first, "gx", ring_x)
         west = lax.ppermute(last, "gx", up_x)
 
     with jax.named_scope("transport"):
         solved, velocity, send = call(
             main_kernel,
             [f32(NZ * ROWS, LANES), f32(2, ROWS, LANES), f32(LANES, LANES)],
-            low, high, south, north, west, east, fields, rows, every, conduct_level,
+            own_one, own_two, one, two, west, east, fields, rows, every, conduct_level,
             conduct_col, geothermal, drag, surface_enthalpy, melt_level, ice_mask, basin,
             owner_slot.reshape(2, LANES), enthalpy.reshape(NZ * ROWS, LANES),
             places="aaaavvaa" + "v" + "a" * 10 + "aaa",

time: 81.1 us -> 76.6 us (0.945)
  starting transfers between devices: 38.2 us -> 30.6 us
  waiting for transfers between devices: 16.4 us -> 19 us
    all_to_all x1, waiting for transfers between devices: 2.18 us -> 7.75 us  [per_device(): every = lax.all_to_all(sums.reshape(LANES, COPIES, LANES), both, 0, 0)]
    all_to_all x1, starting transfers between devices: 11.2 us -> 7.55 us  [per_device(): every = lax.all_to_all(sums.reshape(LANES, COPIES, LANES), both, 0, 0)]
    ppermute x3, waiting for transfers between devices: 3.3 us -> 0.01 us  [the longest x1 0.01 us: per_device(): one = lax.ppermute(one, 'gy', [(i, i ^ 1) for i in range(ny)])]
    ppermute x1, starting transfers between devices: 4.87 us -> 1.64 us  [per_device(): west = lax.ppermute(last, 'gx', up_x)]
    all_to_all x1, starting transfers between devices: 8.71 us -> 6.48 us  [per_device(): received = lax.all_to_all(send.reshape(LANES, 1, LANES), both, 0, 0)]
    ppermute x3, starting transfers between devices: 5.37 us -> 6.86 us  [the longest x1 6.77 us: per_device(): lax.ppermute(two, 'gy', [(i, i if i in ends else (i + 1 ^ 1) - 1) for i i...]
  transfers between devices with their start and end apart: 8 -> 8, of which waited for: 5 -> 3; matrix products, arithmetic and copies ran while one was open for 0% -> 0% of each run, Pallas kernels for 9% -> 9%
where the time goes in v2:
time: 76.6 us; the launch traced here: 75.8 us
  starting transfers between devices  30.6 us (40%)
  Pallas kernels  23.3 us (30%)
  waiting for transfers between devices  19 us (25%)
  local copies, waits for them, and re-layouts  1.53 us (2%)
  between operations  0.78 us (1%)
    pallas_call x7, Pallas kernels, call(): pl.pallas_call(kernel, out_shape=outs, in_specs=specs[:len(args)], out_sp...  23.3 us
    all_to_all x1, waiting for transfers between devices, per_device(): received = lax.all_to_all(send.reshape(LANES, 1, LANES), both, 0, 0)  8.44 us
    all_to_all x1, waiting for transfers between devices, per_device(): every = lax.all_to_all(sums.reshape(LANES, COPIES, LANES), both, 0, 0)  7.75 us
    all_to_all x1, starting transfers between devices, per_device(): every = lax.all_to_all(sums.reshape(LANES, COPIES, LANES), both, 0, 0)  7.55 us
    ppermute x1, starting transfers between devices, per_device(): rows = lax.ppermute(fields, 'gy', ring_y)  7.11 us
    ppermute x1, starting transfers between devices, per_device(): lax.ppermute(two, 'gy', [(i, i if i in ends else (i + 1 ^ 1) - 1) for i i...  6.77 us
    all_to_all x1, starting transfers between devices, per_device(): received = lax.all_to_all(send.reshape(LANES, 1, LANES), both, 0, 0)  6.48 us
    ppermute x1, waiting for transfers between devices, per_device(): edge = lax.ppermute(message, 'gx', ring_x)  2.83 us
  transfers between devices with their start and end apart: 8, of which 3 were waited for; matrix products, arithmetic and copies ran while one was open for 0% of the time, Pallas kernels for 9%

profile of v2, /device:TPU:1, one launch (start us, length us, event | category | flops | bytes accessed | tf_op | source)
XLA Modules:
  0.0 75.8 jit_solution(2036877872844380500)
XLA Ops:
  0.6 1.5 %fields.1.f_ref.f_hbm = f32[10,8,128]{2,1,0:T(8,128)} custom-call(f32[2,16,128]{2,1,0:T(8,128)} %stress_ref.1, f32[16,128]{1,0:T(8,128)} %visc_ref.1, f32[16,128]{1,0:T(8,128)} %drag_ref.3), custom_call_target="tpu_custom_call" | custom-call | bytes 73728 | tf_op jit(solution)/shard_map/fields/pallas_call | solution.py:47
  2.1 0.0 copy-start
  2.1 7.1 %collective-permute-start = (f32[10,8,128]{2,1,0:T(8,128)}, f32[10,8,128]{2,1,0:T(8,128)S(1)}, u32[]{:S(2)}, u32[]{:S(2)}) collective-permute-start(f32[10,8,128]{2,1,0:T(8,128)} %fields.1.f_ref.f_hbm), channel_id=1, source_target_pairs={{1,0},{2,1},{3,2},{4,3},{5,4},{6,5},{7,6},{8,7},{9,8},{10,9},{11,1... | collective-permute-start | bytes 122888 | tf_op jit(solution)/shard_map/fields/ppermute | solution.py:634
  9.2 3.1 %levels_on_lanes.1 = (f32[8,168,128]{2,1,0:T(8,128)}, f32[8,168,128]{2,1,0:T(8,128)}, f32[32,8,128]{2,1,0:T(8,128)}, f32[32,8,128]{2,1,0:T(8,128)}) custom-call(f32[160,16,128]{2,1,0:T(8,128)} %e_ref.1, f32[10,8,128]{2,1,0:T(8,128)} %fields.1.f_ref.f_hbm), custom_call_target="tpu_custom_call" | custom-call | bytes 2990080 | tf_op jit(solution)/shard_map/levels_on_lanes/pallas_call | solution.py:47
  12.3 0.0 collective-permute-done.y_ref.y_hbm
  12.3 0.0 copy-done
  12.3 0.0 copy-start.1
  12.3 0.1 collective-permute-start.1
  12.4 6.8 %collective-permute-start.2 = (f32[8,168,128]{2,1,0:T(8,128)}, f32[8,168,128]{2,1,0:T(8,128)}, u32[]{:S(2)}, u32[]{:S(2)}) collective-permute-start(f32[8,168,128]{2,1,0:T(8,128)} %get-tuple-element.19.own_two), channel_id=1, source_target_pairs={{0,0},{1,2},{2,1},{3,4},{4,3},{5,6},{6,5},{7,8},{8,7},{9,10},{10,9... | collective-permute-start | bytes 2064392 | tf_op jit(solution)/shard_map/halo/ppermute | solution.py:660
  19.2 1.0 %collective-permute-start.3 = (f32[2,8,128]{2,1,0:T(8,128)S(1)}, f32[2,8,128]{2,1,0:T(8,128)S(1)}, u32[]{:S(2)}, u32[]{:S(2)}) collective-permute-start(f32[2,8,128]{2,1,0:T(8,128)S(1)} %moments.2), channel_id=1, source_target_pairs={{16,0},{32,16},{48,32},{64,48},{80,64},{96,80},{112,96},{0,112},{1... | collective-permute-start | bytes 24584 | tf_op jit(solution)/shard_map/moments/ppermute | solution.py:650
  20.2 2.8 %collective-permute-done.3.x_ref = f32[2,8,128]{2,1,0:T(8,128)S(1)} collective-permute-done((f32[2,8,128]{2,1,0:T(8,128)S(1)}, f32[2,8,128]{2,1,0:T(8,128)S(1)}, u32[]{:S(2)}, u32[]{:S(2)}) %collective-permute-start.3) | collective-permute-done | bytes 8224 | tf_op jit(solution)/shard_map/moments/ppermute | solution.py:650
  23.0 1.2 %moments.3 = f32[512,128]{1,0:T(8,128)} custom-call(f32[10,8,128]{2,1,0:T(8,128)S(1)} %copy-done, f32[10,8,128]{2,1,0:T(8,128)S(1)} %collective-permute-done.y_ref.y_hbm, f32[2,8,128]{2,1,0:T(8,128)S(1)} %collective-permute-done.3.x_ref), custom_call_target="tpu_custom_call" | custom-call | bytes 352256 | tf_op jit(solution)/shard_map/moments/pallas_call | solution.py:47
  24.2 7.5 %all-to-all-start = ((f32[128,4,128]{2,1,0:T(4,128)}), f32[128,4,128]{2,1,0:T(4,128)S(1)}, u32[]{:S(2)}, u32[]{:S(2)}) async-start(f32[128,4,128]{2,1,0:T(4,128)} %bitcast), calls=%async_computation | async-start | bytes 524288 | tf_op jit(solution)/shard_map/moments/all_to_all | solution.py:665
  31.7 0.0 collective-permute-done.1.one_hbm.one_ref
  31.7 0.0 collective-permute-done.2.two_hbm.two_ref
  31.7 0.0 copy-done.1
  31.7 2.0 %halo.1 = (f32[43,8,128]{2,1,0:T(8,128)}, f32[43,8,128]{2,1,0:T(8,128)}) custom-call(f32[32,8,128]{2,1,0:T(8,128)} %get-tuple-element.22.own_first, f32[32,8,128]{2,1,0:T(8,128)} %get-tuple-element.23.own_last, f32[10,8,128]{2,1,0:T(8,128)} %fields.1.f_ref.f_hbm, f32[10,8,128]{2,1,0:T(8,128)} %copy-done.1, ...), custom_call_target="tpu_custom_call" | custom-call | tf_op jit(solution)/shard_map/halo/pallas_call | solution.py:47
  33.8 1.6 %collective-permute-start.4 = (f32[43,8,128]{2,1,0:T(8,128)}, f32[43,8,128]{2,1,0:T(8,128)S(1)}, u32[]{:S(2)}, u32[]{:S(2)}) collective-permute-start(f32[43,8,128]{2,1,0:T(8,128)} %get-tuple-element.24), channel_id=1, source_target_pairs={{0,16},{16,32},{32,48},{48,64},{64,80},{80,96},{96,112},{112,0},{1... | collective-permute-start | bytes 528392 | tf_op jit(solution)/shard_map/halo/ppermute | solution.py:680
  35.4 0.0 collective-permute-start.5
  35.4 7.7 %all-to-all-done = f32[128,4,128]{2,1,0:T(4,128)S(1)} async-done(((f32[128,4,128]{2,1,0:T(4,128)}), f32[128,4,128]{2,1,0:T(4,128)S(1)}, u32[]{:S(2)}, u32[]{:S(2)}) %all-to-all-start) | async-done | bytes 262176 | tf_op jit(solution)/shard_map/moments/all_to_all | solution.py:665
  43.2 0.0 copy-start.3
  43.2 0.0 collective-permute-done.4.w_ref
  43.2 0.0 copy-start.4
  43.2 0.0 collective-permute-done.5.x_ref
  43.2 0.0 copy-start.5
  43.2 0.7 copy-done.3
  43.9 0.1 copy-done.4
  43.9 0.1 copy-done.5
  44.0 15.0 %transport.1 = (f32[2560,128]{1,0:T(8,128)}, f32[2,16,128]{2,1,0:T(8,128)}, f32[128,128]{1,0:T(8,128)}) custom-call(f32[8,168,128]{2,1,0:T(8,128)} %get-tuple-element.18.own_one, f32[8,168,128]{2,1,0:T(8,128)} %get-tuple-element.19.own_two, f32[8,168,128]{2,1,0:T(8,128)} %collective-permute-done.1.one_hbm.one_ref, ...), custom_call_target="tpu_custom_call" | custom-call | bytes 6211200 | tf_op jit(solution)/shard_map/transport/pallas_call | solution.py:47
  59.0 6.5 %all-to-all-start.1 = ((f32[128,1,128]{2,1,0:T(1,128)}), f32[128,1,128]{2,1,0:T(1,128)S(1)}, u32[]{:S(2)}, u32[]{:S(2)}) async-start(f32[128,1,128]{2,1,0:T(1,128)} %bitcast.12), calls=%async_computation.1 | async-start | bytes 131072 | tf_op jit(solution)/shard_map/basin_melt/all_to_all | solution.py:710
  65.5 0.0 copy-start.2
  65.5 0.7 copy-done.2
  66.2 0.6 basin_melt.1
  66.8 8.4 %all-to-all-done.1 = f32[128,1,128]{2,1,0:T(1,128)S(1)} async-done(((f32[128,1,128]{2,1,0:T(1,128)}), f32[128,1,128]{2,1,0:T(1,128)S(1)}, u32[]{:S(2)}, u32[]{:S(2)}) %all-to-all-start.1) | async-done | bytes 65568 | tf_op jit(solution)/shard_map/basin_melt/all_to_all | solution.py:710
  75.3 0.5 slice_reduce_fusion
  (1 shorter events, 0.0 us)
Async XLA Ops:
  2.1 10.2 %copy-start = (f32[10,8,128]{2,1,0:T(8,128)S(1)}, f32[10,8,128]{2,1,0:T(8,128)}, u32[]{:S(2)}) copy-start(f32[10,8,128]{2,1,0:T(8,128)} %fields.1.f_ref.f_hbm) | copy-start | bytes 122884
  2.1 10.2 %collective-permute-start = (f32[10,8,128]{2,1,0:T(8,128)}, f32[10,8,128]{2,1,0:T(8,128)S(1)}, u32[]{:S(2)}, u32[]{:S(2)}) collective-permute-start(f32[10,8,128]{2,1,0:T(8,128)} %fields.1.f_ref.f_hbm), channel_id=1, source_target_pairs={{1,0},{2,1},{3,2},{4,3},{5,4},{6,5},{7,6},{8,7},{9,8},{10,9},{11,1... | collective-permute-start | bytes 122888 | tf_op jit(solution)/shard_map/fields/ppermute | solution.py:634
  12.3 19.4 %copy-start.1 = (f32[10,8,128]{2,1,0:T(8,128)}, f32[10,8,128]{2,1,0:T(8,128)S(1)}, u32[]{:S(2)}) copy-start(f32[10,8,128]{2,1,0:T(8,128)S(1)} %collective-permute-done.y_ref.y_hbm) | copy-start | bytes 122884
  12.3 19.4 %collective-permute-start.1 = (f32[8,168,128]{2,1,0:T(8,128)}, f32[8,168,128]{2,1,0:T(8,128)}, u32[]{:S(2)}, u32[]{:S(2)}) collective-permute-start(f32[8,168,128]{2,1,0:T(8,128)} %get-tuple-element.18.own_one), channel_id=1, source_target_pairs={{0,1},{1,0},{2,3},{3,2},{4,5},{5,4},{6,7},{7,6},{8,9},{9,8},{10,11... | collective-permute-start | bytes 2064392 | tf_op jit(solution)/shard_map/halo/ppermute | solution.py:658
  12.4 19.3 %collective-permute-start.2 = (f32[8,168,128]{2,1,0:T(8,128)}, f32[8,168,128]{2,1,0:T(8,128)}, u32[]{:S(2)}, u32[]{:S(2)}) collective-permute-start(f32[8,168,128]{2,1,0:T(8,128)} %get-tuple-element.19.own_two), channel_id=1, source_target_pairs={{0,0},{1,2},{2,1},{3,4},{4,3},{5,6},{6,5},{7,8},{8,7},{9,10},{10,9... | collective-permute-start | bytes 2064392 | tf_op jit(solution)/shard_map/halo/ppermute | solution.py:660
  19.2 3.8 %collective-permute-start.3 = (f32[2,8,128]{2,1,0:T(8,128)S(1)}, f32[2,8,128]{2,1,0:T(8,128)S(1)}, u32[]{:S(2)}, u32[]{:S(2)}) collective-permute-start(f32[2,8,128]{2,1,0:T(8,128)S(1)} %moments.2), channel_id=1, source_target_pairs={{16,0},{32,16},{48,32},{64,48},{80,64},{96,80},{112,96},{0,112},{1... | collective-permute-start | bytes 24584 | tf_op jit(solution)/shard_map/moments/ppermute | solution.py:650
  24.2 19.0 %all-to-all-start = ((f32[128,4,128]{2,1,0:T(4,128)}), f32[128,4,128]{2,1,0:T(4,128)S(1)}, u32[]{:S(2)}, u32[]{:S(2)}) async-start(f32[128,4,128]{2,1,0:T(4,128)} %bitcast), calls=%async_computation | async-start | bytes 524288 | tf_op jit(solution)/shard_map/moments/all_to_all | solution.py:665
  33.8 9.4 %collective-permute-start.4 = (f32[43,8,128]{2,1,0:T(8,128)}, f32[43,8,128]{2,1,0:T(8,128)S(1)}, u32[]{:S(2)}, u32[]{:S(2)}) collective-permute-start(f32[43,8,128]{2,1,0:T(8,128)} %get-tuple-element.24), channel_id=1, source_target_pairs={{0,16},{16,32},{32,48},{48,64},{64,80},{80,96},{96,112},{112,0},{1... | collective-permute-start | bytes 528392 | tf_op jit(solution)/shard_map/halo/ppermute | solution.py:680
  35.4 7.8 %collective-permute-start.5 = (f32[43,8,128]{2,1,0:T(8,128)}, f32[43,8,128]{2,1,0:T(8,128)S(1)}, u32[]{:S(2)}, u32[]{:S(2)}) collective-permute-start(f32[43,8,128]{2,1,0:T(8,128)} %get-tuple-element.25), channel_id=1, source_target_pairs={{16,0},{32,16},{48,32},{64,48},{80,64},{96,80},{112,96},{0,112},{1... | collective-permute-start | bytes 528392 | tf_op jit(solution)/shard_map/halo/ppermute | solution.py:679
  43.2 0.7 copy-start.3
  43.2 0.8 %copy-start.4 = (f32[43,8,128]{2,1,0:T(8,128)}, f32[43,8,128]{2,1,0:T(8,128)S(1)}, u32[]{:S(2)}) copy-start(f32[43,8,128]{2,1,0:T(8,128)S(1)} %collective-permute-done.4.w_ref) | copy-start | bytes 528388
  43.2 0.8 %copy-start.5 = (f32[43,8,128]{2,1,0:T(8,128)}, f32[43,8,128]{2,1,0:T(8,128)S(1)}, u32[]{:S(2)}) copy-start(f32[43,8,128]{2,1,0:T(8,128)S(1)} %collective-permute-done.5.x_ref) | copy-start | bytes 528388
  59.0 16.3 %all-to-all-start.1 = ((f32[128,1,128]{2,1,0:T(1,128)}), f32[128,1,128]{2,1,0:T(1,128)S(1)}, u32[]{:S(2)}, u32[]{:S(2)}) async-start(f32[128,1,128]{2,1,0:T(1,128)} %bitcast.12), calls=%async_computation.1 | async-start | bytes 131072 | tf_op jit(solution)/shard_map/basin_melt/all_to_all | solution.py:710
  65.5 0.7 copy-start.2

commit v3 on v2

--- a/solution.py
+++ b/solution.py
@@ -155,7 +155,6 @@
     def send(src, dst):
         stores.append(start_copy(src, dst, out_sems.at[len(stores)]))
 
-    rows = [ref.at[:, pl.ds(0, NZ), :] for ref in (one_ref, two_ref)]
     for h in range(2):
         loads[h].wait()
         for y in range(8):
@@ -170,7 +169,10 @@
             last[8 * h + y] = wide[120:]
             first[16 + 8 * h + y] = bands[:8]
             last[16 + 8 * h + y] = bands[24:]
-        send(out.at[h], (rows[1 - h], rows[h]))
+            if y % 2 == 1:
+                at = pl.ds(y - 1, 2)
+                dst = [ref.at[at, pl.ds(0, NZ), :] for ref in (one_ref, two_ref)]
+                send(out.at[h, at], (dst[1 - h], dst[h]))
     loads[2].wait()
     send(fields, one_ref.at[:, pl.ds(NZ, 8), :])
     send(fields, two_ref.at[:, pl.ds(NZ, 8), :])
@@ -401,13 +403,13 @@
     krylov_basis(own_f, west_f, east_f, south_f, north_f, basis, turned)
 
     def courants(i, s):
-        for j in range(53):
-            k = NZ - 1 - (i * 53 + j)
-            lower = col * lev[k - 1]
-            one = 1.0 / (s + lower)
-            inv[rows_at(k * ROWS, ROWS), :] = one
-            s = 1.0 + lower * (s * one)
         for j in range(6):
+            for p in range(9 * j, min(9 * j + 9, 53)):
+                k = NZ - 1 - (i * 53 + p)
+                lower = col * lev[k - 1]
+                one = 1.0 / (s + lower)
+                inv[rows_at(k * ROWS, ROWS), :] = one
+                s = 1.0 + lower * (s * one)
             at = rows_at((i * 6 + j) * 8, 8)
             for comp, o_ref in ((0, wide_x), (1, wide_y)):
                 v = c[0] * turned[comp, 0, at, :]
@@ -490,13 +492,13 @@
     for s in range(1, STEPS):
 
         def tiles(i, carry, s=s):
-            for j in range(6):
-                substep(wide, wide_x, wide_y, s, i * 6 + j)
-            for j in range(2):
-                substep(band, band_x, band_y, s, i * 2 + j)
+            for j in range(9):
+                substep(wide, wide_x, wide_y, s, i * 9 + j)
+            for j in range(3):
+                substep(band, band_x, band_y, s, i * 3 + j)
             return carry
 
-        lax.fori_loop(0, 3, tiles, 0)
+        lax.fori_loop(0, 2, tiles, 0)
 
     def last_step(buf, cx_ref, cy_ref, y, t):
         src, at = (STEPS - 1) % 2, 8 * t
@@ -639,7 +641,7 @@
             enthalpy, fields, places="aa" + "aaaa",
             scratch=(
                 vmem(2, NZ, 8, LANES), vmem(2, 8, NZ, LANES), vmem(8, 8, LANES),
-                vmem(32, 8, LANES), vmem(32, 8, LANES), dma((3,)), dma((6,)),
+                vmem(32, 8, LANES), vmem(32, 8, LANES), dma((3,)), dma((12,)),
             ),
             limit=FULL,
         )

time: 76.6 us -> 76.6 us (level)
  no operation moved by 1% of the time
where the time goes in v3:
time: 76.6 us; the launch traced here: 75.8 us
  starting transfers between devices  30.7 us (40%)
  Pallas kernels  23.2 us (30%)
  waiting for transfers between devices  19 us (25%)
  local copies, waits for them, and re-layouts  1.53 us (2%)
  between operations  0.78 us (1%)
    pallas_call x7, Pallas kernels, call(): pl.pallas_call(kernel, out_shape=outs, in_specs=specs[:len(args)], out_sp...  23.2 us
    all_to_all x1, waiting for transfers between devices, per_device(): received = lax.all_to_all(send.reshape(LANES, 1, LANES), both, 0, 0)  8.44 us
    all_to_all x1, waiting for transfers between devices, per_device(): every = lax.all_to_all(sums.reshape(LANES, COPIES, LANES), both, 0, 0)  7.75 us
    all_to_all x1, starting transfers between devices, per_device(): every = lax.all_to_all(sums.reshape(LANES, COPIES, LANES), both, 0, 0)  7.68 us
    ppermute x1, starting transfers between devices, per_device(): rows = lax.ppermute(fields, 'gy', ring_y)  7.11 us
    ppermute x1, starting transfers between devices, per_device(): lax.ppermute(two, 'gy', [(i, i if i in ends else (i + 1 ^ 1) - 1) for i i...  6.77 us
    all_to_all x1, starting transfers between devices, per_device(): received = lax.all_to_all(send.reshape(LANES, 1, LANES), both, 0, 0)  6.48 us
    ppermute x1, waiting for transfers between devices, per_device(): edge = lax.ppermute(message, 'gx', ring_x)  2.83 us
  transfers between devices with their start and end apart: 8, of which 3 were waited for; matrix products, arithmetic and copies ran while one was open for 0% of the time, Pallas kernels for 9%

profile of v3, /device:TPU:1, one launch (start us, length us, event | category | flops | bytes accessed | tf_op | source)
XLA Modules:
  0.0 75.8 jit_solution(8103701634891113214)
XLA Ops:
  0.6 1.5 %fields.1.f_ref.f_hbm = f32[10,8,128]{2,1,0:T(8,128)} custom-call(f32[2,16,128]{2,1,0:T(8,128)} %stress_ref.1, f32[16,128]{1,0:T(8,128)} %visc_ref.1, f32[16,128]{1,0:T(8,128)} %drag_ref.3), custom_call_target="tpu_custom_call" | custom-call | bytes 73728 | tf_op jit(solution)/shard_map/fields/pallas_call | solution.py:47
  2.1 0.0 copy-start
  2.1 7.1 %collective-permute-start = (f32[10,8,128]{2,1,0:T(8,128)}, f32[10,8,128]{2,1,0:T(8,128)S(1)}, u32[]{:S(2)}, u32[]{:S(2)}) collective-permute-start(f32[10,8,128]{2,1,0:T(8,128)} %fields.1.f_ref.f_hbm), channel_id=1, source_target_pairs={{1,0},{2,1},{3,2},{4,3},{5,4},{6,5},{7,6},{8,7},{9,8},{10,9},{11,1... | collective-permute-start | bytes 122888 | tf_op jit(solution)/shard_map/fields/ppermute | solution.py:636
  9.2 3.0 %levels_on_lanes.1 = (f32[8,168,128]{2,1,0:T(8,128)}, f32[8,168,128]{2,1,0:T(8,128)}, f32[32,8,128]{2,1,0:T(8,128)}, f32[32,8,128]{2,1,0:T(8,128)}) custom-call(f32[160,16,128]{2,1,0:T(8,128)} %e_ref.1, f32[10,8,128]{2,1,0:T(8,128)} %fields.1.f_ref.f_hbm), custom_call_target="tpu_custom_call" | custom-call | bytes 2990080 | tf_op jit(solution)/shard_map/levels_on_lanes/pallas_call | solution.py:47
  12.2 0.0 collective-permute-done.y_ref.y_hbm
  12.2 0.0 copy-done
  12.2 0.0 copy-start.1
  12.2 0.1 collective-permute-start.1
  12.3 6.8 %collective-permute-start.2 = (f32[8,168,128]{2,1,0:T(8,128)}, f32[8,168,128]{2,1,0:T(8,128)}, u32[]{:S(2)}, u32[]{:S(2)}) collective-permute-start(f32[8,168,128]{2,1,0:T(8,128)} %get-tuple-element.19.own_two), channel_id=1, source_target_pairs={{0,0},{1,2},{2,1},{3,4},{4,3},{5,6},{6,5},{7,8},{8,7},{9,10},{10,9... | collective-permute-start | bytes 2064392 | tf_op jit(solution)/shard_map/halo/ppermute | solution.py:662
  19.1 1.0 %collective-permute-start.3 = (f32[2,8,128]{2,1,0:T(8,128)S(1)}, f32[2,8,128]{2,1,0:T(8,128)S(1)}, u32[]{:S(2)}, u32[]{:S(2)}) collective-permute-start(f32[2,8,128]{2,1,0:T(8,128)S(1)} %moments.2), channel_id=1, source_target_pairs={{16,0},{32,16},{48,32},{64,48},{80,64},{96,80},{112,96},{0,112},{1... | collective-permute-start | bytes 24584 | tf_op jit(solution)/shard_map/moments/ppermute | solution.py:652
  20.0 2.8 %collective-permute-done.3.x_ref = f32[2,8,128]{2,1,0:T(8,128)S(1)} collective-permute-done((f32[2,8,128]{2,1,0:T(8,128)S(1)}, f32[2,8,128]{2,1,0:T(8,128)S(1)}, u32[]{:S(2)}, u32[]{:S(2)}) %collective-permute-start.3) | collective-permute-done | bytes 8224 | tf_op jit(solution)/shard_map/moments/ppermute | solution.py:652
  22.9 1.2 %moments.3 = f32[512,128]{1,0:T(8,128)} custom-call(f32[10,8,128]{2,1,0:T(8,128)S(1)} %copy-done, f32[10,8,128]{2,1,0:T(8,128)S(1)} %collective-permute-done.y_ref.y_hbm, f32[2,8,128]{2,1,0:T(8,128)S(1)} %collective-permute-done.3.x_ref), custom_call_target="tpu_custom_call" | custom-call | bytes 352256 | tf_op jit(solution)/shard_map/moments/pallas_call | solution.py:47
  24.0 7.7 %all-to-all-start = ((f32[128,4,128]{2,1,0:T(4,128)}), f32[128,4,128]{2,1,0:T(4,128)S(1)}, u32[]{:S(2)}, u32[]{:S(2)}) async-start(f32[128,4,128]{2,1,0:T(4,128)} %bitcast), calls=%async_computation | async-start | bytes 524288 | tf_op jit(solution)/shard_map/moments/all_to_all | solution.py:667
  31.7 0.0 collective-permute-done.1.one_hbm.one_ref
  31.7 0.0 collective-permute-done.2.two_hbm.two_ref
  31.7 0.0 copy-done.1
  31.7 2.0 %halo.1 = (f32[43,8,128]{2,1,0:T(8,128)}, f32[43,8,128]{2,1,0:T(8,128)}) custom-call(f32[32,8,128]{2,1,0:T(8,128)} %get-tuple-element.22.own_first, f32[32,8,128]{2,1,0:T(8,128)} %get-tuple-element.23.own_last, f32[10,8,128]{2,1,0:T(8,128)} %fields.1.f_ref.f_hbm, f32[10,8,128]{2,1,0:T(8,128)} %copy-done.1, ...), custom_call_target="tpu_custom_call" | custom-call | tf_op jit(solution)/shard_map/halo/pallas_call | solution.py:47
  33.8 1.6 %collective-permute-start.4 = (f32[43,8,128]{2,1,0:T(8,128)}, f32[43,8,128]{2,1,0:T(8,128)S(1)}, u32[]{:S(2)}, u32[]{:S(2)}) collective-permute-start(f32[43,8,128]{2,1,0:T(8,128)} %get-tuple-element.24), channel_id=1, source_target_pairs={{0,16},{16,32},{32,48},{48,64},{64,80},{80,96},{96,112},{112,0},{1... | collective-permute-start | bytes 528392 | tf_op jit(solution)/shard_map/halo/ppermute | solution.py:682
  35.4 0.0 collective-permute-start.5
  35.4 7.7 %all-to-all-done = f32[128,4,128]{2,1,0:T(4,128)S(1)} async-done(((f32[128,4,128]{2,1,0:T(4,128)}), f32[128,4,128]{2,1,0:T(4,128)S(1)}, u32[]{:S(2)}, u32[]{:S(2)}) %all-to-all-start) | async-done | bytes 262176 | tf_op jit(solution)/shard_map/moments/all_to_all | solution.py:667
  43.2 0.0 copy-start.3
  43.2 0.0 collective-permute-done.4.w_ref
  43.2 0.0 copy-start.4
  43.2 0.0 collective-permute-done.5.x_ref
  43.2 0.0 copy-start.5
  43.2 0.7 copy-done.3
  43.9 0.1 copy-done.4
  43.9 0.1 copy-done.5
  44.0 15.0 %transport.1 = (f32[2560,128]{1,0:T(8,128)}, f32[2,16,128]{2,1,0:T(8,128)}, f32[128,128]{1,0:T(8,128)}) custom-call(f32[8,168,128]{2,1,0:T(8,128)} %get-tuple-element.18.own_one, f32[8,168,128]{2,1,0:T(8,128)} %get-tuple-element.19.own_two, f32[8,168,128]{2,1,0:T(8,128)} %collective-permute-done.1.one_hbm.one_ref, ...), custom_call_target="tpu_custom_call" | custom-call | bytes 6211200 | tf_op jit(solution)/shard_map/transport/pallas_call | solution.py:47
  59.0 6.5 %all-to-all-start.1 = ((f32[128,1,128]{2,1,0:T(1,128)}), f32[128,1,128]{2,1,0:T(1,128)S(1)}, u32[]{:S(2)}, u32[]{:S(2)}) async-start(f32[128,1,128]{2,1,0:T(1,128)} %bitcast.12), calls=%async_computation.1 | async-start | bytes 131072 | tf_op jit(solution)/shard_map/basin_melt/all_to_all | solution.py:712
  65.5 0.0 copy-start.2
  65.5 0.7 copy-done.2
  66.2 0.6 basin_melt.1
  66.8 8.4 %all-to-all-done.1 = f32[128,1,128]{2,1,0:T(1,128)S(1)} async-done(((f32[128,1,128]{2,1,0:T(1,128)}), f32[128,1,128]{2,1,0:T(1,128)S(1)}, u32[]{:S(2)}, u32[]{:S(2)}) %all-to-all-start.1) | async-done | bytes 65568 | tf_op jit(solution)/shard_map/basin_melt/all_to_all | solution.py:712
  75.3 0.5 slice_reduce_fusion
  (1 shorter events, 0.0 us)
Async XLA Ops:
  2.1 10.1 %copy-start = (f32[10,8,128]{2,1,0:T(8,128)S(1)}, f32[10,8,128]{2,1,0:T(8,128)}, u32[]{:S(2)}) copy-start(f32[10,8,128]{2,1,0:T(8,128)} %fields.1.f_ref.f_hbm) | copy-start | bytes 122884
  2.1 10.1 %collective-permute-start = (f32[10,8,128]{2,1,0:T(8,128)}, f32[10,8,128]{2,1,0:T(8,128)S(1)}, u32[]{:S(2)}, u32[]{:S(2)}) collective-permute-start(f32[10,8,128]{2,1,0:T(8,128)} %fields.1.f_ref.f_hbm), channel_id=1, source_target_pairs={{1,0},{2,1},{3,2},{4,3},{5,4},{6,5},{7,6},{8,7},{9,8},{10,9},{11,1... | collective-permute-start | bytes 122888 | tf_op jit(solution)/shard_map/fields/ppermute | solution.py:636
  12.2 19.5 %copy-start.1 = (f32[10,8,128]{2,1,0:T(8,128)}, f32[10,8,128]{2,1,0:T(8,128)S(1)}, u32[]{:S(2)}) copy-start(f32[10,8,128]{2,1,0:T(8,128)S(1)} %collective-permute-done.y_ref.y_hbm) | copy-start | bytes 122884
  12.2 19.5 %collective-permute-start.1 = (f32[8,168,128]{2,1,0:T(8,128)}, f32[8,168,128]{2,1,0:T(8,128)}, u32[]{:S(2)}, u32[]{:S(2)}) collective-permute-start(f32[8,168,128]{2,1,0:T(8,128)} %get-tuple-element.18.own_one), channel_id=1, source_target_pairs={{0,1},{1,0},{2,3},{3,2},{4,5},{5,4},{6,7},{7,6},{8,9},{9,8},{10,11... | collective-permute-start | bytes 2064392 | tf_op jit(solution)/shard_map/halo/ppermute | solution.py:660
  12.3 19.4 %collective-permute-start.2 = (f32[8,168,128]{2,1,0:T(8,128)}, f32[8,168,128]{2,1,0:T(8,128)}, u32[]{:S(2)}, u32[]{:S(2)}) collective-permute-start(f32[8,168,128]{2,1,0:T(8,128)} %get-tuple-element.19.own_two), channel_id=1, source_target_pairs={{0,0},{1,2},{2,1},{3,4},{4,3},{5,6},{6,5},{7,8},{8,7},{9,10},{10,9... | collective-permute-start | bytes 2064392 | tf_op jit(solution)/shard_map/halo/ppermute | solution.py:662
  19.1 3.8 %collective-permute-start.3 = (f32[2,8,128]{2,1,0:T(8,128)S(1)}, f32[2,8,128]{2,1,0:T(8,128)S(1)}, u32[]{:S(2)}, u32[]{:S(2)}) collective-permute-start(f32[2,8,128]{2,1,0:T(8,128)S(1)} %moments.2), channel_id=1, source_target_pairs={{16,0},{32,16},{48,32},{64,48},{80,64},{96,80},{112,96},{0,112},{1... | collective-permute-start | bytes 24584 | tf_op jit(solution)/shard_map/moments/ppermute | solution.py:652
  24.0 19.1 %all-to-all-start = ((f32[128,4,128]{2,1,0:T(4,128)}), f32[128,4,128]{2,1,0:T(4,128)S(1)}, u32[]{:S(2)}, u32[]{:S(2)}) async-start(f32[128,4,128]{2,1,0:T(4,128)} %bitcast), calls=%async_computation | async-start | bytes 524288 | tf_op jit(solution)/shard_map/moments/all_to_all | solution.py:667
  33.8 9.4 %collective-permute-start.4 = (f32[43,8,128]{2,1,0:T(8,128)}, f32[43,8,128]{2,1,0:T(8,128)S(1)}, u32[]{:S(2)}, u32[]{:S(2)}) collective-permute-start(f32[43,8,128]{2,1,0:T(8,128)} %get-tuple-element.24), channel_id=1, source_target_pairs={{0,16},{16,32},{32,48},{48,64},{64,80},{80,96},{96,112},{112,0},{1... | collective-permute-start | bytes 528392 | tf_op jit(solution)/shard_map/halo/ppermute | solution.py:682
  35.4 7.8 %collective-permute-start.5 = (f32[43,8,128]{2,1,0:T(8,128)}, f32[43,8,128]{2,1,0:T(8,128)S(1)}, u32[]{:S(2)}, u32[]{:S(2)}) collective-permute-start(f32[43,8,128]{2,1,0:T(8,128)} %get-tuple-element.25), channel_id=1, source_target_pairs={{16,0},{32,16},{48,32},{64,48},{80,64},{96,80},{112,96},{0,112},{1... | collective-permute-start | bytes 528392 | tf_op jit(solution)/shard_map/halo/ppermute | solution.py:681
  43.2 0.7 copy-start.3
  43.2 0.8 %copy-start.4 = (f32[43,8,128]{2,1,0:T(8,128)}, f32[43,8,128]{2,1,0:T(8,128)S(1)}, u32[]{:S(2)}) copy-start(f32[43,8,128]{2,1,0:T(8,128)S(1)} %collective-permute-done.4.w_ref) | copy-start | bytes 528388
  43.2 0.8 %copy-start.5 = (f32[43,8,128]{2,1,0:T(8,128)}, f32[43,8,128]{2,1,0:T(8,128)S(1)}, u32[]{:S(2)}) copy-start(f32[43,8,128]{2,1,0:T(8,128)S(1)} %collective-permute-done.5.x_ref) | copy-start | bytes 528388
  59.0 16.3 %all-to-all-start.1 = ((f32[128,1,128]{2,1,0:T(1,128)}), f32[128,1,128]{2,1,0:T(1,128)S(1)}, u32[]{:S(2)}, u32[]{:S(2)}) async-start(f32[128,1,128]{2,1,0:T(1,128)} %bitcast.12), calls=%async_computation.1 | async-start | bytes 131072 | tf_op jit(solution)/shard_map/basin_melt/all_to_all | solution.py:712
  65.5 0.7 copy-start.2
